TPU v7x, 256 devices: a whole 4x4x8 slice. The times are simulated.
256 devices in a mesh: region: 8 (over z_hi, core), tile: 32 (over y, x, z_lo).
Axes of the slice: x: 4, y: 4, z: 8 (z_hi: 4, z_lo: 2; z = z_hi * 2 + z_lo), core: 2. Of those that a mesh axis runs over, the one named last changes fastest.
Arguments:
- tangent: float32 [8, 32, 2, 64, 900], P('region', 'tile'), may hold values from -6 to 6
- adjoint: float32 [8, 32, 2, 64, 900], P('region', 'tile'), may hold values from -6 to 6
- reference_uppermost_tracers: float32 [8, 32, 2, 900], P('region', 'tile'), may hold values from -1 to 1.5
- velocity: float32 [8, 32, 2, 64, 900], P('region', 'tile'), may hold values from -1.5 to 1.5
- kappa: float32 [8, 32, 63, 900], P('region', 'tile'), may hold values from 0.025 to 1600
- depth_levels: int32 [8, 32, 900], P('region', 'tile'), may hold values from 0 to 64
- forcing: float32 [8, 131072], P(None, 'region'), may hold values from -4 to 4
- forcing_point: int32 [8, 32, 900], P('region', 'tile'), may hold values from 0 to 131071
- partner_edge: int32 [8, 32, 4], P('region', 'tile'), may hold values from 0 to 127, as said below
- edge_flip: int32 [8, 32, 4], P('region', 'tile'), may hold values from 0 to 1
Outputs:
- tangent_next: float32 [8, 32, 2, 64, 900], P('region', 'tile')
- adjoint_prev: float32 [8, 32, 2, 64, 900], P('region', 'tile')
Inputs may be any that keep to these rules, and one draw needn't show every extreme that they name: partner_edge[r, t, s] names an edge of the same region; partner of partner is the edge itself, no edge names itself, and edge_flip agrees on both edges of a pair. The side 0 edge of each slot pairs with the side 1 edge of the same slot. Every side 2 edge pairs with the side 2 edge of another slot, and every side 3 edge pairs with the side 3 edge of another slot.
All inputs are finite; a program needn't handle non-finite values.
Results may differ from a plain program's by a relative error of at most 0.0003.
Values sent between devices are 32-bit elements; how exact they have to be, the bound alone decides.
No kernel may reach another device: no remote copies, remote signals or barrier semaphores. Data moves between devices by JAX's collectives and lax.ppermute only.
A program may use at most 192 MiB of HBM per device.

v0:
```python
import jax
import jax.numpy as jnp
from jax import lax
from jax.sharding import PartitionSpec as P

SIDE = 30
Z = 64


diffusion = 0.2


def grid_masks():
    position = jnp.arange(SIDE * SIDE, dtype=jnp.int32)
    return (position % SIDE, position // SIDE)


def edge_rows(west_src, east_src, south_src, north_src):
    slot_count = west_src.shape[0]
    shaped = lambda source: source.reshape(slot_count, 2 * Z, SIDE, SIDE)
    stacked = jnp.stack(
        [
            shaped(west_src)[:, :, :, 0],
            shaped(east_src)[:, :, :, SIDE - 1],
            shaped(south_src)[:, :, 0, :],
            shaped(north_src)[:, :, SIDE - 1, :],
        ],
        axis=1,
    )
    return jnp.transpose(stacked, (0, 1, 3, 2)).reshape(slot_count * 4, SIDE, 2 * Z)


def take_partner(gathered, partner_edge, edge_flip):
    slot_count = partner_edge.shape[0]
    chosen = jnp.take(gathered, partner_edge.reshape(-1), axis=0)
    flipped = jnp.where(edge_flip.reshape(-1)[:, None, None] == 1, chosen[:, ::-1, :], chosen)
    return jnp.transpose(flipped.reshape(slot_count, 4, SIDE, 2 * Z), (0, 1, 3, 2)).reshape(
        slot_count, 4, 2, Z, SIDE
    )


def spread(rim_values):
    west_full = jnp.repeat(rim_values[:, 0], SIDE, axis=-1)
    east_full = jnp.repeat(rim_values[:, 1], SIDE, axis=-1)
    south_full = jnp.tile(rim_values[:, 2], (1, 1, 1, SIDE))
    north_full = jnp.tile(rim_values[:, 3], (1, 1, 1, SIDE))
    return (west_full, east_full, south_full, north_full)


def horizontal(tracer, rim_values, velocity, wetness):
    column, row_index = grid_masks()
    west_full, east_full, south_full, north_full = spread(rim_values)
    from_east = jnp.where(column == SIDE - 1, east_full, jnp.roll(tracer, -1, axis=-1))
    from_west = jnp.where(column == 0, west_full, jnp.roll(tracer, 1, axis=-1))
    from_north = jnp.where(row_index == SIDE - 1, north_full, jnp.roll(tracer, -SIDE, axis=-1))
    from_south = jnp.where(row_index == 0, south_full, jnp.roll(tracer, SIDE, axis=-1))
    along_x = velocity[:, 0:1]
    along_y = velocity[:, 1:2]
    mixed_terms = (
        (1.0 - 4.0 * diffusion) * tracer
        + (diffusion - 0.5 * along_x) * from_east
        + (diffusion + 0.5 * along_x) * from_west
    )
    mixed_terms = (
        mixed_terms
        + (diffusion - 0.5 * along_y) * from_north
        + (diffusion + 0.5 * along_y) * from_south
    )
    return wetness * mixed_terms


def surface_terms(reference_uppermost_tracers, forcing_cells, uppermost_ocean_indicator):
    (
        wind_east,
        wind_north,
        air_temp,
        moisture_content,
        precipitation_amount,
        continental_discharge,
        pressure,
        ice_cover,
    ) = [forcing_cells[number] for number in range(8)]
    airflow_magnitude = jnp.sqrt(wind_east * wind_east + wind_north * wind_north + 1.0)
    seawater_mass_per_volume = jnp.exp(0.3 * (pressure - air_temp))
    icefree_share = 1.0 / (1.0 + jnp.exp(ice_cover))
    transported_quantity = icefree_share * seawater_mass_per_volume * airflow_magnitude
    vapour_capacity_moisture = jnp.exp(0.5 * reference_uppermost_tracers[:, 0] - 0.2 * pressure)
    vapour_capacity_derivative = 0.5 * vapour_capacity_moisture
    precipitation_minus_evaporation = (
        0.5 * transported_quantity * (vapour_capacity_moisture - moisture_content)
        - precipitation_amount
        - continental_discharge
    )
    thermal_diagonal_coupling = (
        -(0.5 * transported_quantity + 0.5 * transported_quantity * vapour_capacity_derivative)
        * uppermost_ocean_indicator
    )
    haline_thermal_coupling = (
        0.5
        * reference_uppermost_tracers[:, 1]
        * transported_quantity
        * vapour_capacity_derivative
        * uppermost_ocean_indicator
    )
    salt_self = precipitation_minus_evaporation * uppermost_ocean_indicator
    return (thermal_diagonal_coupling, haline_thermal_coupling, salt_self)


def vertical_solve(right_side, coupling):
    slot_count = right_side.shape[0]
    edge_zero = jnp.zeros((slot_count, 1, SIDE * SIDE), jnp.float32)
    upper_link = jnp.concatenate([edge_zero, coupling], axis=1)
    lower_link = jnp.concatenate([coupling, edge_zero], axis=1)
    centre = 1.0 + upper_link + lower_link
    stacked = (
        jnp.moveaxis(centre, 1, 0)[:, :, None],
        jnp.moveaxis(upper_link, 1, 0)[:, :, None],
        jnp.moveaxis(lower_link, 1, 0)[:, :, None],
        jnp.moveaxis(right_side, 2, 0),
    )

    def eliminate(carry, inputs):
        factor_prev, partial_prev = carry
        centre_here, upper_here, lower_here, right_here = inputs
        divisor = centre_here + upper_here * factor_prev
        factor = -lower_here / divisor
        partial_value = (right_here + upper_here * partial_prev) / divisor
        return ((factor, partial_value), (factor, partial_value))

    initial = (
        jnp.zeros((slot_count, 1, SIDE * SIDE), jnp.float32),
        jnp.zeros((slot_count, 2, SIDE * SIDE), jnp.float32),
    )
    unused, (factors, partials) = lax.scan(eliminate, initial, stacked)

    def substitute(carry, inputs):
        factor, partial_value = inputs
        result = partial_value - factor * carry
        return (result, result)

    unused_last, solved = lax.scan(
        substitute,
        jnp.zeros((slot_count, 2, SIDE * SIDE), jnp.float32),
        (factors, partials),
        reverse=True,
    )
    return jnp.moveaxis(solved, 0, 2)


def adjoint_pushes(solved, velocity, wetness):
    column, row_index = grid_masks()
    weighted = wetness * solved
    along_x = velocity[:, 0:1]
    along_y = velocity[:, 1:2]
    push_east = (diffusion - 0.5 * along_x) * weighted
    push_west = (diffusion + 0.5 * along_x) * weighted
    push_north = (diffusion - 0.5 * along_y) * weighted
    push_south = (diffusion + 0.5 * along_y) * weighted
    inner = (1.0 - 4.0 * diffusion) * weighted
    inner = inner + jnp.where(column != 0, jnp.roll(push_east, 1, axis=-1), 0.0)
    inner = inner + jnp.where(column != SIDE - 1, jnp.roll(push_west, -1, axis=-1), 0.0)
    inner = inner + jnp.where(row_index != 0, jnp.roll(push_north, SIDE, axis=-1), 0.0)
    inner = inner + jnp.where(row_index != SIDE - 1, jnp.roll(push_south, -SIDE, axis=-1), 0.0)
    outward = edge_rows(push_west, push_east, push_south, push_north)
    return (inner, outward)


def adjoint_finish(
    inner, incoming, solved, wetness, thermal_diagonal_coupling, haline_thermal_coupling, salt_self
):
    column, row_index = grid_masks()
    west_full, east_full, south_full, north_full = spread(incoming)
    total = (
        inner
        + jnp.where(column == 0, west_full, 0.0)
        + jnp.where(column == SIDE - 1, east_full, 0.0)
    )
    total = (
        total
        + jnp.where(row_index == 0, south_full, 0.0)
        + jnp.where(row_index == SIDE - 1, north_full, 0.0)
    )
    top_heat = (
        thermal_diagonal_coupling * solved[:, 0, 0] + haline_thermal_coupling * solved[:, 1, 0]
    )
    top_salt = salt_self * solved[:, 1, 0]
    total = total.at[:, 0, 0].add(top_heat).at[:, 1, 0].add(top_salt)
    return wetness * total


def shards(
    tangent,
    adjoint,
    reference_uppermost_tracers,
    velocity,
    kappa,
    depth_levels,
    forcing,
    forcing_point,
    partner_edge,
    edge_flip,
):
    tangent = tangent[0]
    adjoint = adjoint[0]
    reference_uppermost_tracers = reference_uppermost_tracers[0]
    velocity = velocity[0]
    kappa = kappa[0]
    depth_levels = depth_levels[0]
    forcing_point = forcing_point[0]
    partner_edge = partner_edge[0]
    edge_flip = edge_flip[0]
    levels = jnp.arange(Z, dtype=jnp.int32)
    wet_levels = (levels[None, :, None] < depth_levels[:, None, :]).astype(jnp.float32)
    wetness = wet_levels[:, None]
    coupling = kappa * wet_levels[:, :-1] * wet_levels[:, 1:]
    masked = tangent * wetness
    tangent_edges = edge_rows(masked, masked, masked, masked)
    whole_forcing = lax.all_gather(forcing, "region", axis=1, tiled=True)
    forcing_cells = jnp.take(whole_forcing, forcing_point, axis=1)
    gathered_edges = lax.all_gather(tangent_edges, "tile", axis=0, tiled=True)
    tangent_rims = take_partner(gathered_edges, partner_edge, edge_flip)
    right_side = horizontal(masked, tangent_rims, velocity, wetness)
    solved = vertical_solve(adjoint, coupling)
    inner, outward = adjoint_pushes(solved, velocity, wetness)
    gathered_out = lax.all_gather(outward, "tile", axis=0, tiled=True)
    incoming = take_partner(gathered_out, partner_edge, edge_flip)
    thermal_diagonal_coupling, haline_thermal_coupling, salt_self = surface_terms(
        reference_uppermost_tracers, forcing_cells, wet_levels[:, 0]
    )
    top_heat = thermal_diagonal_coupling * masked[:, 0, 0]
    top_salt = haline_thermal_coupling * masked[:, 0, 0] + salt_self * masked[:, 1, 0]
    right_side = right_side.at[:, 0, 0].add(top_heat).at[:, 1, 0].add(top_salt)
    tangent_next = vertical_solve(right_side, coupling)
    adjoint_prev = adjoint_finish(
        inner,
        incoming,
        solved,
        wetness,
        thermal_diagonal_coupling,
        haline_thermal_coupling,
        salt_self,
    )
    return (tangent_next[None], adjoint_prev[None])


def solution(mesh):
    in_specs = (
        P("region", "tile", None, None, None),
        P("region", "tile", None, None, None),
        P("region", "tile", None, None),
        P("region", "tile", None, None, None),
        P("region", "tile", None, None),
        P("region", "tile", None),
        P(None, "region"),
        P("region", "tile", None),
        P("region", "tile", None),
        P("region", "tile", None),
    )
    out_specs = (P("region", "tile", None, None, None), P("region", "tile", None, None, None))
    return jax.shard_map(shards, mesh=mesh, in_specs=in_specs, out_specs=out_specs, check_vma=False)
```

profile of v0, /device:TPU:6, one launch (start us, length us, event | category | flops | bytes accessed | tf_op | source)
XLA Modules:
  0.0 1112.9 jit_solution(16774513435479999644)
XLA Ops:
  12.0 42.0 %while.74 = (s32[]{:T(128)}, f32[1,1,900]{2,1,0:T(1,128)S(1)}, f32[1,2,900]{2,1,0:T(2,128)S(1)}, f32[64,1,1,900]{3,2,1,0:T(1,128)}, f32[64,1,2,900]{3,2,1,0:T(2,...) while((s32[]{:T(128)}, f32[1,1,900]{2,1,0:T(1,128)S(1)}, ...), condition=%wide.region_5.7_spmd.clone, body=%wide.region_4.6_spmd.clone.sunk | while | flops 11703 | bytes 70892 | solution.py:134
  54.1 55.9 %while.75 = (s32[]{:T(128)}, f32[1,2,900]{2,1,0:T(2,128)S(1)}, f32[64,1,2,900]{3,0,2,1:T(8,128)S(1)}, f32[64,1,2,900]{3,2,1,0:T(2,128)S(1)}, f32[64,1,1,900]{3,2...) while((s32[]{:T(128)}, f32[1,2,900]{2,1,0:T(2,128)S(1)}, f32[64,1,2,900]{3,0,2,1:T(8,128)S(1)}, ...), condition=%wide.region_7.9_spmd.clone, body=%wide.region_6.8_spmd.clone.sunk | while | flops 5404 | bytes 61319 | solution.py:141
  112.7 2.9 reshape.1279
  116.8 2.9 reshape.1280
  121.0 2.9 reshape.1281
  123.9 2.2 copy.161
  126.1 2.9 reshape.1282
  133.5 2.3 mul.673
  135.7 2.9 mul.740
  138.6 2.9 squeeze.102
  141.6 1.6 mul.675
  144.2 5.7 copy.152
  150.9 1.8 slice.384
  163.4 121.8 %all-gather.10.cloned.1.call-done = f32[1,128,30,128]{3,0,2,1:T(1,128)} async-done(((f32[1,4,30,128]{3,0,2,1:T(1,128)}), f32[1,128,30,128]{3,0,2,1:T(1,128)}) %all-gather.10.cloned.1.call-update) | async-done | bytes 1966096 | tf_op jit(solution)/shard_map/all_gather | solution.py:225
  285.2 3.1 copy.187
  288.4 2.1 gather_fusion.2
  290.5 153.4 %all-gather.8.cloned.1.call-done = f32[1,128,30,128]{3,0,2,1:T(1,128)} async-done(((f32[1,4,30,128]{3,0,2,1:T(1,128)}), f32[1,128,30,128]{3,0,2,1:T(1,128)}) %all-gather.8.cloned.1.call-update) | async-done | bytes 1966096 | tf_op jit(solution)/shard_map/all_gather | solution.py:220
  443.9 3.1 copy.188
  447.1 2.1 gather_fusion.1
  470.1 3.5 fusion.23
  476.0 547.4 %all-gather.6.cloned.1.call-done = f32[8,131072]{0,1:T(8,128)} async-done(((f32[8,16384]{0,1:T(8,128)}), f32[8,131072]{0,1:T(8,128)}) %all-gather.6.cloned.1.call-update) | async-done | bytes 4194320 | tf_op jit(solution)/shard_map/all_gather | solution.py:218
  1023.4 14.5 %gather_fusion = f32[900,8]{1,0:T(8,128)S(1)} fusion(f32[8,131072]{0,1:T(8,128)} %all-gather.6.cloned.1.call-done, s32[1024]{0:T(1024)S(1)} %pad_clamp_fusion), kind=kCustom, calls=%fused_computation.2 | custom fusion | bytes 61200 | tf_op jit(solution)/shard_map/jit(_take)/gather | solution.py:219
  1041.2 51.0 %while.72 = (s32[]{:T(128)}, f32[1,1,900]{2,1,0:T(1,128)S(1)}, f32[1,2,900]{2,1,0:T(2,128)S(1)}, f32[64,1,1,900]{3,2,1,0:T(1,128)S(1)}, f32[64,1,2,900]{3,2,1,0:...) while((s32[]{:T(128)}, f32[1,1,900]{2,1,0:T(1,128)S(1)}, ...), condition=%wide.region_1.3_spmd.clone, body=%wide.region_0.0_spmd.clone.sunk | while | flops 11703 | bytes 86772 | solution.py:134
  1092.2 13.3 %while.73 = (s32[]{:T(128)}, f32[1,2,900]{2,1,0:T(2,128)S(1)}, f32[64,1,2,900]{3,0,2,1:T(8,128)S(1)}, f32[64,1,2,900]{3,2,1,0:T(2,128)S(1)}, f32[64,1,1,900]{3,2...) while((s32[]{:T(128)}, f32[1,2,900]{2,1,0:T(2,128)S(1)}, f32[64,1,2,900]{3,0,2,1:T(8,128)S(1)}, ...), condition=%wide.region_3.5_spmd.clone, body=%wide.region_2.4_spmd.clone.sunk | while | flops 5404 | bytes 61319 | solution.py:141
  (992 shorter events, 208.8 us)
Async XLA Ops:
  7.2 278.0 %all-gather.10.cloned.1.call-start = ((), (), s32[]{:S(2)}) async-start(), calls=%async_computation.2 | async-start | bytes 2027520 | tf_op jit(solution)/shard_map/all_gather | solution.py:225
  10.2 99.9 %copy-start.18 = (f32[1,1,2,64,900]{4,3,2,1,0:T(8,128)S(1)}, f32[1,1,2,64,900]{4,3,2,1,0:T(8,128)}, u32[]{:S(2)}) copy-start(f32[1,1,2,64,900]{4,3,2,1,0:T(8,128)} %param.31) | copy-start | bytes 1382404
  11.0 99.2 %copy-start = (f32[1,1,2,64,900]{4,3,2,1,0:T(8,128)S(1)}, f32[1,1,2,64,900]{4,3,2,1,0:T(8,128)}, u32[]{:S(2)}) copy-start(f32[1,1,2,64,900]{4,3,2,1,0:T(8,128)} %param.28) | copy-start | bytes 1382404
  54.0 56.2 %copy-start.21 = (f32[64,1,1,900]{3,2,1,0:T(1,128)}, f32[64,1,1,900]{3,2,1,0:T(1,128)S(1)}, u32[]{:S(2)}) copy-start(f32[64,1,1,900]{3,2,1,0:T(1,128)S(1)} %get-tuple-element.956) | copy-start | bytes 691204
  54.0 56.2 %copy-start.22 = (f32[64,1,1,900]{3,2,1,0:T(1,128)}, f32[64,1,1,900]{3,2,1,0:T(1,128)S(1)}, u32[]{:S(2)}) copy-start(f32[64,1,1,900]{3,2,1,0:T(1,128)S(1)} %get-tuple-element.957) | copy-start | bytes 691204
  54.0 56.2 %copy-start.23 = (f32[64,1,1,900]{3,2,1,0:T(1,128)}, f32[64,1,1,900]{3,2,1,0:T(1,128)S(1)}, u32[]{:S(2)}) copy-start(f32[64,1,1,900]{3,2,1,0:T(1,128)S(1)} %get-tuple-element.958) | copy-start | bytes 691204
  131.2 312.7 %all-gather.8.cloned.1.call-start = ((), (), s32[]{:S(2)}) async-start(), calls=%async_computation.1 | async-start | bytes 2027520 | tf_op jit(solution)/shard_map/all_gather | solution.py:220
  144.0 879.4 %all-gather.6.cloned.1.call-start = ((), (), s32[]{:S(2)}) async-start(), calls=%async_computation | async-start | bytes 75497472 | tf_op jit(solution)/shard_map/all_gather | solution.py:218
  149.9 8.0 copy-start.29
  469.9 3.7 copy-start.6
  470.0 3.7 copy-start.8
  470.0 3.7 copy-start.10
  470.0 3.9 copy-start.12
  470.0 4.1 copy-start.13
  470.0 4.3 copy-start.14
  470.0 4.7 copy-start.15
  470.0 4.9 copy-start.16
  470.0 5.2 copy-start.17
  470.1 5.2 copy-start.24
  470.1 5.2 copy-start.25
  470.1 5.2 copy-start.26
  470.1 5.3 copy-start.27
  475.3 562.7 %copy-start.31 = (pred[900]{0:T(1024)(128)(4,1)S(1)}, pred[900]{0:T(1024)(128)(4,1)}, u32[]{:S(2)}) copy-start(pred[900]{0:T(1024)(128)(4,1)} %compare_and_fusion) | copy-start | bytes 2704
  475.3 562.8 %copy-start.28 = (f32[1,1,2,900]{3,2,1,0:T(2,128)S(1)}, f32[1,1,2,900]{3,2,1,0:T(2,128)}, u32[]{:S(2)}) copy-start(f32[1,1,2,900]{3,2,1,0:T(2,128)} %param.30) | copy-start | bytes 21604
  (12 other events, 29.2 us)
Sparse Core Ops, SparseCore 0:
  131.3 153.8 all-gather.9
  287.0 156.8 all-gather.7
  445.8 577.5 all-gather.5
where the time goes:
time: 1130 us; the launch traced here: 1110 us
  waiting for transfers between devices  823 us (73%)
  local copies, waits for them, and re-layouts  156 us (14%)
  other arithmetic  112 us (10%)
  between operations  14.4 us (1%)
    all_gather x1, waiting for transfers between devices, shards(): whole_forcing = lax.all_gather(forcing, 'region', axis=1, tiled=True)  547 us
    all_gather x1, waiting for transfers between devices, shards(): gathered_edges = lax.all_gather(tangent_edges, 'tile', axis=0, tiled=True)  153 us
    all_gather x1, waiting for transfers between devices, shards(): gathered_out = lax.all_gather(outward, 'tile', axis=0, tiled=True)  122 us
    dynamic_update_slice x256, other arithmetic, vertical_solve(): unused, (factors, partials) = lax.scan(eliminate, initial, stacked)  89.6 us
    dynamic_slice x192, local copies, waits for them, and re-layouts, vertical_solve(): unused, (factors, partials) = lax.scan(eliminate, initial, stacked)  45.6 us
  transfers between devices with their start and end apart: 3, of which 3 were waited for; matrix products, arithmetic and copies ran while one was open for 6% of the time, Pallas kernels for 0%

commit v1 on v0

v1 whole, which is shorter than its diff:
```python
import jax
import jax.numpy as jnp
from jax import lax
from jax.experimental import pallas as pl
from jax.experimental.pallas import tpu as pltpu
from jax.sharding import PartitionSpec as P

SIDE = 30
Z = 64
CELLS = SIDE * SIDE
WIDE = 1024
CHUNKS = WIDE // 128
GROUPS = Z // 8
D = 0.2
CENTRE = 1.0 - 4.0 * D
F32 = jnp.float32
VMEM_LIMIT = 48 * 1024 * 1024


def lanes(rows, width=WIDE):
    return lax.broadcasted_iota(jnp.int32, (rows, width), 1)


def split(row):
    return [row[:, 128 * c : 128 * c + 128] for c in range(CHUNKS)]


def roll(value, shift):
    return pltpu.roll(value, shift % value.shape[-1], value.ndim - 1)


def grid_masks(rows=1):
    cell = lanes(rows)
    y = lax.shift_right_logical(cell * 2185, 16)
    x = cell - y * SIDE
    return x == 0, x == SIDE - 1, y == 0, y == SIDE - 1


def mirrored(value):
    back = 127 - lanes(value.shape[0], 128)
    parts = [jnp.take_along_axis(part, back, axis=1) for part in split(value)]
    return roll(jnp.concatenate(parts[::-1], axis=1), CELLS)


def table_kernel(forcing_ref, table_ref):
    wu, wv, ta, qa, pr, ro, ps, ic = [
        forcing_ref[pl.ds(field, 128, stride=8), :] for field in range(8)
    ]
    speed = jnp.sqrt(wu * wu + wv * wv + 1.0)
    carrier = jnp.exp(0.3 * (ps - ta)) * speed / (1.0 + jnp.exp(ic))
    table_ref[0:128, :] = carrier
    table_ref[128:256, :] = carrier * jnp.exp(-0.2 * ps)
    table_ref[256:384, :] = 0.5 * carrier * qa + pr + ro


def lookup_kernel(own_ref, mate_ref, q0, q1, q2, q3, a0, a1, a2, a3, pieces, ask):
    band = lax.axis_index("region")
    for number, ref in enumerate((own_ref, mate_ref)):
        value = ref[...]
        coarse = value.astype(jnp.bfloat16)
        pieces[384 * number : 384 * number + 384, 0:128] = coarse
        pieces[384 * number : 384 * number + 384, 128:256] = (
            value - coarse.astype(F32)
        ).astype(jnp.bfloat16)
    base_own = band * 128
    base_mate = (band + 1 - 2 * lax.rem(band, 2)) * 128
    low = jnp.bitwise_and(lax.broadcasted_iota(jnp.int32, (256, 256), 0), 127)
    high = lax.broadcasted_iota(jnp.int32, (128, 256), 0)
    for q_ref, a_ref in ((q0, a0), (q1, a1), (q2, a2), (q3, a3)):
        ask[...] = jnp.zeros((1, WIDE), jnp.int32)
        ask[:, 0:CELLS] = q_ref[0]
        for part in range(4):
            point = ask[:, 256 * part : 256 * part + 256]
            onehot = (low == jnp.bitwise_and(point, 127)).astype(jnp.bfloat16)
            found = jnp.dot(pieces[...], onehot, preferred_element_type=F32)
            row = lax.shift_right_logical(point, 7)
            here = high == row - base_own
            there = high == row - base_mate
            for field in range(3):
                picked = jnp.where(here, found[128 * field : 128 * field + 128], 0.0)
                picked = picked + jnp.where(
                    there, found[384 + 128 * field : 512 + 128 * field], 0.0
                )
                total = jnp.sum(picked, axis=0, keepdims=True)
                at = 8 * field + 2 * part
                a_ref[at : at + 1, :] = total[:, 0:128]
                a_ref[at + 1 : at + 2, :] = total[:, 128:256]


def main_kernel(
    partner_ref, flip_ref, tan_ref, adj_ref, vel_ref, kap_ref, depth_ref,
    edge_ref, rhs_ref, back_ref, rim_ref, top_ref, link_ref, inv_ref,
    coup, given, part, solved,
):
    cell = lanes(1)
    depth = jnp.where(cell < CELLS, depth_ref[...], 0)
    sub = lax.broadcasted_iota(jnp.int32, (8, WIDE), 0)

    def relayout(i, carry):
        rows = pl.ds(pl.multiple_of(8 * i, 8), 8)
        level = sub + 8 * i
        link = jnp.where(level + 1 < depth, kap_ref[rows, :], 0.0)
        at = pl.multiple_of(64 * i, 64)
        sources = (link, adj_ref[0, rows, :], adj_ref[1, rows, :])
        for target, value in enumerate(sources):
            for c, piece in enumerate(split(value)):
                where = pl.ds(at + 8 * c, 8)
                if target == 0:
                    coup[where, :] = piece
                else:
                    given[target - 1, where, :] = piece
        return carry

    lax.fori_loop(0, GROUPS, relayout, 0)

    def forward(i, carry):
        e, y_t, y_s, m = carry
        for s in range(8):
            strided = pl.ds(64 * i + s, 8, stride=8)
            packed = pl.ds(pl.multiple_of(64 * i + 8 * s, 8), 8)
            link = coup[strided, :]
            inv = 1.0 / (e + link)
            y_t = given[0, strided, :] + m * y_t
            y_s = given[1, strided, :] + m * y_s
            m = link * inv
            e = 1.0 + m * e
            inv_ref[packed, :] = inv
            link_ref[packed, :] = m
            part[0, packed, :] = y_t * inv
            part[1, packed, :] = y_s * inv
        return e, y_t, y_s, m

    zero = jnp.zeros((8, 128), F32)
    lax.fori_loop(0, GROUPS, forward, (zero + 1.0, zero, zero, zero))

    def backward(n, carry):
        x_t, x_s = carry
        i = GROUPS - 1 - n
        for s in reversed(range(8)):
            strided = pl.ds(64 * i + s, 8, stride=8)
            packed = pl.ds(pl.multiple_of(64 * i + 8 * s, 8), 8)
            m = link_ref[packed, :]
            x_t = part[0, packed, :] + m * x_t
            x_s = part[1, packed, :] + m * x_s
            solved[0, strided, :] = x_t
            solved[1, strided, :] = x_s
        return x_t, x_s

    x_t, x_s = lax.fori_loop(0, GROUPS, backward, (zero, zero))
    top_ref[16:24, :] = x_t
    top_ref[24:32, :] = x_s

    x0, x29, y0, y29 = grid_masks(8)
    turned = jnp.full((8, WIDE), flip_ref[0, 0] == 1)
    small = lanes(8, 128)
    south, north = flip_ref[0, 2] == 1, flip_ref[0, 3] == 1
    order = small
    for first, turn in ((0, south), (30, north), (60, south), (90, north)):
        inside = jnp.logical_and(small >= first, small < first + SIDE)
        order = jnp.where(
            jnp.logical_and(inside, turn), 2 * first + SIDE - 1 - small, order
        )

    def stencil(i, carry):
        rows = pl.ds(pl.multiple_of(8 * i, 8), 8)
        at = pl.multiple_of(64 * i, 64)
        wet = sub + 8 * i < depth
        half_x, half_y = 0.5 * vel_ref[0, rows, :], 0.5 * vel_ref[1, rows, :]
        to_e, to_w, to_n, to_s = D - half_x, D + half_x, D - half_y, D + half_y
        for t in range(2):
            value = jnp.where(wet, tan_ref[t, rows, :], 0.0)
            image = mirrored(value)
            east = jnp.where(
                x29, jnp.where(turned, image, roll(value, 29)), roll(value, -1)
            )
            west = jnp.where(
                x0, jnp.where(turned, image, roll(value, -29)), roll(value, 1)
            )
            northern = jnp.where(y29, 0.0, roll(value, -SIDE))
            southern = jnp.where(y0, 0.0, roll(value, SIDE))
            mixed = CENTRE * value + to_e * east + to_w * west
            mixed = jnp.where(wet, mixed + to_n * northern + to_s * southern, 0.0)
            for c, piece in enumerate(split(mixed)):
                rhs_ref[t, pl.ds(at + 8 * c, 8), :] = piece

            answer = jnp.concatenate(
                [solved[t, pl.ds(at + 8 * c, 8), :] for c in range(CHUNKS)], axis=1
            )
            answer = jnp.where(wet, answer, 0.0)
            push_e = jnp.where(wet, to_e * answer, 0.0)
            push_w = jnp.where(wet, to_w * answer, 0.0)
            push_n = jnp.where(wet, to_n * answer, 0.0)
            push_s = jnp.where(wet, to_s * answer, 0.0)
            crossing = jnp.where(x29, push_e, push_w)
            image = mirrored(crossing)
            inner = CENTRE * answer
            inner = inner + jnp.where(
                x0, jnp.where(turned, image, roll(crossing, -29)), roll(push_e, 1)
            )
            inner = inner + jnp.where(
                x29, jnp.where(turned, image, roll(crossing, 29)), roll(push_w, -1)
            )
            inner = inner + jnp.where(y0, 0.0, roll(push_n, SIDE))
            inner = inner + jnp.where(y29, 0.0, roll(push_s, -SIDE))
            inner = jnp.where(wet, inner, 0.0)
            for c, piece in enumerate(split(inner)):
                back_ref[t, pl.ds(at + 8 * c, 8), :] = piece

            value, push_s, push_n = split(value), split(push_s), split(push_n)
            upper = small >= 102
            edges = jnp.where(small < 30, value[0], 0.0)
            packs = (
                (roll(jnp.where(upper, value[6], value[7]), 56), 30),
                (roll(push_s[0], 60), 60),
                (roll(jnp.where(upper, push_n[6], push_n[7]), 116), 90),
            )
            for piece, first in packs:
                inside = jnp.logical_and(small >= first, small < first + SIDE)
                edges = jnp.where(inside, piece, edges)
            edges = jnp.take_along_axis(edges, order, axis=1)
            edge_ref[pl.ds(pl.multiple_of(64 * t + 8 * i, 8), 8), :] = edges
        wet, to_n, to_s = split(wet), split(to_n), split(to_s)
        rim = (
            jnp.where(jnp.logical_and(wet[0], small < SIDE), to_s[0], 0.0),
            jnp.where(jnp.logical_and(wet[6], small >= 102), to_n[6], 0.0),
            jnp.where(jnp.logical_and(wet[7], small < 4), to_n[7], 0.0),
        )
        for number, piece in enumerate(rim):
            rim_ref[pl.ds(pl.multiple_of(64 * number + 8 * i, 8), 8), :] = piece
        return carry

    lax.fori_loop(0, GROUPS, stencil, 0)
    wet = 0 < depth
    for t in range(2):
        for c, piece in enumerate(split(jnp.where(wet, tan_ref[t, 0:1, :], 0.0))):
            top_ref[8 * t + c : 8 * t + c + 1, :] = piece
    second = jnp.logical_or(small < 30, jnp.logical_and(small >= 60, small < 90))
    target = jnp.where(
        second,
        lax.shift_right_logical(partner_ref[0, 2], 2),
        lax.shift_right_logical(partner_ref[0, 3], 2),
    )
    edge_ref[128:136, :] = jnp.where(small < 120, target, -1).astype(F32)


def route_kernel(e0, e1, e2, e3, out_ref):
    mine = jnp.bitwise_and(lax.axis_index("tile"), 3)
    sources = (e0, e1, e2, e3)
    goals = [ref[128:129, :].astype(jnp.int32) for ref in sources]
    for b in range(8):
        total = jnp.zeros((128, 128), F32)
        for goal, ref in zip(goals, sources):
            total = jnp.where(goal == 4 * b + mine, ref[0:128, :], total)
        out_ref[b] = total


def finish_kernel(
    edge_ref, rhs_ref, back_ref, rim_ref, top_ref, link_ref, inv_ref,
    r0, r1, r2, r3, depth_ref, base_ref, next_ref, prev_ref,
    right, part, solved, row,
):
    cell = lanes(1)
    depth = jnp.where(cell < CELLS, depth_ref[...], 0)
    for c, piece in enumerate(split(depth)):
        row[0, c : c + 1, :] = piece.astype(F32)
    for t in range(2):
        for c, piece in enumerate(split(base_ref[t : t + 1, :])):
            row[1 + t, c : c + 1, :] = piece
    carrier, scaled, loss = [
        r0[8 * f : 8 * f + 8, :]
        + r1[8 * f : 8 * f + 8, :]
        + r2[8 * f : 8 * f + 8, :]
        + r3[8 * f : 8 * f + 8, :]
        for f in range(3)
    ]
    moist = scaled * jnp.exp(0.5 * row[1])
    wet = row[0] > 0.0
    heat_self = jnp.where(wet, -(0.5 * carrier + 0.25 * moist), 0.0)
    salt_heat = jnp.where(wet, 0.25 * row[2] * moist, 0.0)
    salt_self = jnp.where(wet, 0.5 * moist - loss, 0.0)
    tan_t, tan_s = top_ref[0:8, :], top_ref[8:16, :]
    adj_t, adj_s = top_ref[16:24, :], top_ref[24:32, :]

    small = lanes(8, 128)
    sub = lax.broadcasted_iota(jnp.int32, (8, WIDE), 0)

    def rims(i, carry):
        rows = pl.ds(pl.multiple_of(8 * i, 8), 8)
        at = pl.multiple_of(64 * i, 64)
        wet = split(sub + 8 * i < depth)
        rim = [rim_ref[pl.ds(pl.multiple_of(64 * n + 8 * i, 8), 8), :] for n in range(3)]
        for t in range(2):
            where = pl.ds(pl.multiple_of(64 * t + 8 * i, 8), 8)
            edge = edge_ref[0, where, :]
            for b in range(1, 8):
                edge = edge + edge_ref[b, where, :]
            north = roll(edge, 72)
            from_s, from_n = roll(edge, 68), roll(edge, 12)
            for c in range(CHUNKS):
                put = pl.ds(at + 8 * c, 8)
                value = rhs_ref[t, put, :]
                if c == 0:
                    value = value + rim[0] * edge
                elif c >= 6:
                    value = value + rim[c - 5] * north
                right[t, put, :] = value
                value = back_ref[t, put, :]
                if c == 0:
                    inside = jnp.logical_and(wet[0], small < SIDE)
                    value = value + jnp.where(inside, from_s, 0.0)
                elif c == 6:
                    inside = jnp.logical_and(wet[6], small >= 102)
                    value = value + jnp.where(inside, from_n, 0.0)
                elif c == 7:
                    inside = jnp.logical_and(wet[7], small < 4)
                    value = value + jnp.where(inside, from_n, 0.0)
                prev_ref[t, rows, 128 * c : 128 * c + 128] = value
        return carry

    lax.fori_loop(0, GROUPS, rims, 0)
    zero = jnp.zeros((8, 128), F32)
    first = pl.ds(0, 8, stride=8)
    right[0, first, :] = right[0, first, :] + heat_self * tan_t
    right[1, first, :] = right[1, first, :] + salt_heat * tan_t + salt_self * tan_s
    adds = (heat_self * adj_t + salt_heat * adj_s, salt_self * adj_s)
    for t, add in enumerate(adds):
        for c in range(CHUNKS):
            spot = slice(128 * c, 128 * c + 128)
            prev_ref[t, 0:1, spot] = prev_ref[t, 0:1, spot] + add[c : c + 1, :]

    def forward(i, carry):
        y_t, y_s, m = carry
        for s in range(8):
            strided = pl.ds(64 * i + s, 8, stride=8)
            packed = pl.ds(pl.multiple_of(64 * i + 8 * s, 8), 8)
            y_t = right[0, strided, :] + m * y_t
            y_s = right[1, strided, :] + m * y_s
            m = link_ref[packed, :]
            inv = inv_ref[packed, :]
            part[0, packed, :] = y_t * inv
            part[1, packed, :] = y_s * inv
        return y_t, y_s, m

    lax.fori_loop(0, GROUPS, forward, (zero, zero, zero))

    def backward(n, carry):
        x_t, x_s = carry
        i = GROUPS - 1 - n
        for s in reversed(range(8)):
            strided = pl.ds(64 * i + s, 8, stride=8)
            packed = pl.ds(pl.multiple_of(64 * i + 8 * s, 8), 8)
            m = link_ref[packed, :]
            x_t = part[0, packed, :] + m * x_t
            x_s = part[1, packed, :] + m * x_s
            solved[0, strided, :] = x_t
            solved[1, strided, :] = x_s
        return x_t, x_s

    lax.fori_loop(0, GROUPS, backward, (zero, zero))

    def write(i, carry):
        rows = pl.ds(pl.multiple_of(8 * i, 8), 8)
        at = pl.multiple_of(64 * i, 64)
        for t in range(2):
            for c in range(CHUNKS):
                next_ref[t, rows, 128 * c : 128 * c + 128] = solved[
                    t, pl.ds(at + 8 * c, 8), :
                ]
        return carry

    lax.fori_loop(0, GROUPS, write, 0)


def whole(shape):
    return pl.BlockSpec(shape, lambda _: (0,) * len(shape))


def call(kernel, name, outs, in_shapes, out_shapes, scratch=(), scalars=0):
    specs = [pl.BlockSpec(memory_space=pltpu.SMEM)] * scalars
    specs += [whole(shape) for shape in in_shapes]
    return pl.pallas_call(
        kernel,
        grid=(1,),
        in_specs=specs,
        out_specs=[whole(shape) for shape in out_shapes],
        out_shape=[jax.ShapeDtypeStruct(shape, F32) for shape in outs],
        scratch_shapes=list(scratch),
        compiler_params=pltpu.CompilerParams(vmem_limit_bytes=VMEM_LIMIT),
        name=name,
    )


def shift_chips(value, k):
    return lax.ppermute(value, "region", [(i, (i + 2 * k) % 8) for i in range(8)])


def shards(
    tangent, adjoint, base, velocity, kappa, depth_levels, forcing, forcing_point, partner_edge,
    edge_flip,
):
    tangent, adjoint, velocity = tangent[0, 0], adjoint[0, 0], velocity[0, 0]
    base, kappa, depth = base[0, 0], kappa[0, 0], depth_levels[0]
    natural = (2, Z, WIDE)
    blocked = (2, 8 * Z, 128)
    flat = (8 * Z, 128)

    asked = [forcing_point] + [shift_chips(forcing_point, k) for k in (1, 2, 3)]
    banded = forcing.reshape(8, 128, 128).transpose(1, 0, 2).reshape(1024, 128)
    (table,) = call(
        table_kernel, "tables", [(384, 128)], [(1024, 128)], [(384, 128)]
    )(banded)
    mate = lax.ppermute(table, "region", [(i, i ^ 1) for i in range(8)])

    edges, rhs, back, rim, top, link, inv = call(
        main_kernel,
        "main",
        [(136, 128), blocked, blocked, (192, 128), (32, 128), flat, flat],
        [natural, natural, natural, (Z, WIDE), (1, WIDE)],
        [(136, 128), blocked, blocked, (192, 128), (32, 128), flat, flat],
        [
            pltpu.VMEM(flat, F32),
            pltpu.VMEM(blocked, F32),
            pltpu.VMEM(blocked, F32),
            pltpu.VMEM(blocked, F32),
        ],
        scalars=2,
    )(partner_edge[0], edge_flip[0], tangent, adjoint, velocity, kappa, depth)
    near = [edges] + [
        lax.ppermute(edges, "tile", [(i, i ^ k) for i in range(32)]) for k in (1, 2, 3)
    ]

    answers = call(
        lookup_kernel,
        "lookup",
        [(24, 128)] * 4,
        [(384, 128)] * 2 + [(1, 1, CELLS)] * 4,
        [(24, 128)] * 4,
        [pltpu.VMEM((768, 256), jnp.bfloat16), pltpu.VMEM((1, WIDE), jnp.int32)],
    )(table, mate, *asked)
    replies = [answers[0]] + [shift_chips(answers[k], -k) for k in (1, 2, 3)]

    (slots,) = call(
        route_kernel, "route", [(8, 128, 128)], [(136, 128)] * 4, [(8, 128, 128)]
    )(*near)
    groups = [[4 * b + a for b in range(8)] for a in range(4)]
    arrived = lax.all_to_all(slots, "tile", 0, 0, axis_index_groups=groups, tiled=True)

    following, previous = call(
        finish_kernel,
        "finish",
        [(2, Z, CELLS)] * 2,
        [(8, 128, 128), blocked, blocked, (192, 128), (32, 128), flat, flat]
        + [(24, 128)] * 4
        + [(1, WIDE), (2, WIDE)],
        [natural, natural],
        [
            pltpu.VMEM(blocked, F32),
            pltpu.VMEM(blocked, F32),
            pltpu.VMEM(blocked, F32),
            pltpu.VMEM((3, 8, 128), F32),
        ],
    )(arrived, rhs, back, rim, top, link, inv, *replies, depth, base)
    return following[None, None], previous[None, None]


def solution(mesh):
    fields = P("region", "tile", None, None, None)
    rows = P("region", "tile", None, None)
    single = P("region", "tile", None)
    in_specs = (fields, fields, rows, fields, rows, single, P(None, "region"), single, single, single)
    return jax.shard_map(
        shards, mesh=mesh, in_specs=in_specs, out_specs=(fields, fields), check_vma=False
    )
```

time: 1130 us -> 57 us (0.05); the launches traced: 1110 us -> 56.7 us
  waiting for transfers between devices: 823 us -> 11.2 us
  local copies, waits for them, and re-layouts: 156 us -> 4.32 us
  other arithmetic: 112 us -> 0 us
  starting transfers between devices: 0.3 us -> 28.1 us
  between operations: 14.4 us -> 0.71 us
  Pallas kernels: 0 us -> 12.4 us
    all_gather x3 -> x0, waiting for transfers between devices: 823 us -> none  [the longest x1 547 us: shards(): whole_forcing = lax.all_gather(forcing, 'region', axis=1, tiled=True)]
    dynamic_update_slice x256 -> x0, other arithmetic: 89.6 us -> none  [vertical_solve(): unused, (factors, partials) = lax.scan(eliminate, initial, stacked)]
    dynamic_slice x192 -> x0, local copies, waits for them, and re-layouts: 45.6 us -> none  [vertical_solve(): unused, (factors, partials) = lax.scan(eliminate, initial, stacked)]
    ppermute x0 -> x10, starting transfers between devices: none -> 20.5 us  [the longest x6 16.8 us: shift_chips(): lax.ppermute(value, 'region', [(i, (i + 2 * k) % 8) for i in range(8)])]
    gather x4 -> x0, local copies, waits for them, and re-layouts: 19 us -> none  [the longest x2 14.7 us: shards(): forcing_cells = jnp.take(whole_forcing, forcing_point, axis=1)]
    dynamic_update_slice x256 -> x0, local copies, waits for them, and re-layouts: 16.7 us -> none  [vertical_solve(): unused, (factors, partials) = lax.scan(eliminate, initial, stacked)]
    pallas_call x0 -> x5, Pallas kernels: none -> 12.4 us  [the longest x1 6.55 us: shards(): call(main_kernel, 'main', [(136, 128), blocked, blocked, (192, 128), (32,...]
    another operation x19 -> x0, local copies, waits for them, and re-layouts: 12.2 us -> none  [the longest x5 5.06 us: spread(): south_full = jnp.tile(rim_values[:, 2], (1, 1, 1, SIDE))]
  transfers between devices with their start and end apart: 3 -> 11, of which waited for: 3 -> 6; matrix products, arithmetic and copies ran while one was open for 6% -> 0% of each run, Pallas kernels for 0% -> 5%
where the time goes in v1:
time: 57 us; the launch traced here: 56.7 us
  starting transfers between devices  28.1 us (49%)
  Pallas kernels  12.4 us (22%)
  waiting for transfers between devices  11.2 us (20%)
  local copies, waits for them, and re-layouts  4.32 us (8%)
  between operations  0.71 us (1%)
    ppermute x6, starting transfers between devices, shift_chips(): lax.ppermute(value, 'region', [(i, (i + 2 * k) % 8) for i in range(8)])  16.8 us
    all_to_all x1, starting transfers between devices, shards(): lax.all_to_all(slots, 'tile', 0, 0, axis_index_groups=groups, tiled=True)  7.56 us
    ppermute x6, waiting for transfers between devices, shift_chips(): lax.ppermute(value, 'region', [(i, (i + 2 * k) % 8) for i in range(8)])  7.02 us
    pallas_call x1, Pallas kernels, shards(): call(main_kernel, 'main', [(136, 128), blocked, blocked, (192, 128), (32,...  6.55 us
    unnamed x19, local copies, waits for them, and re-layouts  4.32 us
    ppermute x3, waiting for transfers between devices, shards(): lax.ppermute(edges, 'tile', [(i, i ^ k) for i in range(32)])  4.2 us
    ppermute x3, starting transfers between devices, shards(): lax.ppermute(edges, 'tile', [(i, i ^ k) for i in range(32)])  3.58 us
    pallas_call x1, Pallas kernels, shards(): call(lookup_kernel, 'lookup', [(24, 128)] * 4, [(384, 128)] * 2 + [(1, 1,...  2.68 us
  transfers between devices with their start and end apart: 11, of which 6 were waited for; matrix products, arithmetic and copies ran while one was open for 0% of the time, Pallas kernels for 5%

profile of v1, /device:TPU:6, one launch (start us, length us, event | category | flops | bytes accessed | tf_op | source)
XLA Modules:
  0.0 56.7 jit_solution(14489199309899746151)
XLA Ops:
  0.6 1.1 %copy.14 = f32[1,1,63,900]{3,2,1,0:T(8,128)S(1)} copy(f32[1,1,63,900]{3,1,2,0:T(1,128)} %param.14) | data formatting | bytes 453600
  1.8 0.6 %copy-done.4 = s32[1,1,900]{2,1,0:T(1,128)S(1)} copy-done((s32[1,1,900]{2,1,0:T(1,128)S(1)}, s32[1,1,900]{2,1,0:T(1,128)}, u32[]{:S(2)}) %copy-start.4) | copy-done | bytes 3624
  2.4 1.0 %copy-done.1 = f32[1,1,2,64,900]{4,3,2,1,0:T(8,128)S(1)} copy-done((f32[1,1,2,64,900]{4,3,2,1,0:T(8,128)S(1)}, f32[1,1,2,64,900]{4,3,2,1,0:T(8,128)}, u32[]{:S(2)}) %copy-start.1) | copy-done | bytes 460824
  3.5 1.0 %copy-done.2 = f32[1,1,2,64,900]{4,3,2,1,0:T(8,128)S(1)} copy-done((f32[1,1,2,64,900]{4,3,2,1,0:T(8,128)S(1)}, f32[1,1,2,64,900]{4,3,2,1,0:T(8,128)}, u32[]{:S(2)}) %copy-start.2) | copy-done | bytes 460824
  4.5 6.6 %main.1 = (f32[136,128]{1,0:T(8,128)S(1)}, f32[2,512,128]{2,1,0:T(8,128)S(1)}, f32[2,512,128]{2,1,0:T(8,128)S(1)}, f32[192,128]{1,0:T(8,128)S(1)}, f32[32,128]{1...) custom-call(s32[1,4]{1,0:T(1,128)S(1)} %bitcast.25, s32[1,4]{1,0:T(1,128)S(1)} %bitcast.26, ...), custom_call_target="tpu_custom_call" | custom-call | tf_op jit(solution)/shard_map/main/pallas_call | solution.py:414
  11.1 2.3 %collective-permute-start.2 = (f32[136,128]{1,0:T(8,128)S(1)}, f32[136,128]{1,0:T(8,128)S(1)}, u32[]{:S(2)}, u32[]{:S(2)}) collective-permute-start(f32[136,128]{1,0:T(8,128)S(1)} %get-tuple-element.15.e0), channel_id=1, source_target_pairs={{0,3},{1,2},{2,1},{3,0},{4,7},{5,6},{6,5},{7,4},{8,11},{9,10},{10,... | collective-permute-start | bytes 208904 | tf_op jit(solution)/shard_map/ppermute | solution.py:429
  13.3 1.2 %collective-permute-start.1 = (f32[136,128]{1,0:T(8,128)S(1)}, f32[136,128]{1,0:T(8,128)S(1)}, u32[]{:S(2)}, u32[]{:S(2)}) collective-permute-start(f32[136,128]{1,0:T(8,128)S(1)} %get-tuple-element.15.e0), channel_id=1, source_target_pairs={{0,2},{1,3},{2,0},{3,1},{4,6},{5,7},{6,4},{7,5},{8,10},{9,11},{10,... | collective-permute-start | bytes 208904 | tf_op jit(solution)/shard_map/ppermute | solution.py:429
  14.6 1.8 %collective-permute-done.2.e3 = f32[136,128]{1,0:T(8,128)S(1)} collective-permute-done((f32[136,128]{1,0:T(8,128)S(1)}, f32[136,128]{1,0:T(8,128)S(1)}, u32[]{:S(2)}, u32[]{:S(2)}) %collective-permute-start.2) | collective-permute-done | bytes 69664 | tf_op jit(solution)/shard_map/ppermute | solution.py:429
  16.5 1.3 %collective-permute-done.1.e2 = f32[136,128]{1,0:T(8,128)S(1)} collective-permute-done((f32[136,128]{1,0:T(8,128)S(1)}, f32[136,128]{1,0:T(8,128)S(1)}, u32[]{:S(2)}, u32[]{:S(2)}) %collective-permute-start.1) | collective-permute-done | bytes 69664 | tf_op jit(solution)/shard_map/ppermute | solution.py:429
  17.7 1.1 %collective-permute-done.e1 = f32[136,128]{1,0:T(8,128)S(1)} collective-permute-done((f32[136,128]{1,0:T(8,128)S(1)}, f32[136,128]{1,0:T(8,128)S(1)}, u32[]{:S(2)}, u32[]{:S(2)}) %collective-permute-start) | collective-permute-done | bytes 69664 | tf_op jit(solution)/shard_map/ppermute | solution.py:429
  18.8 0.9 %route.1 = f32[8,128,128]{2,1,0:T(8,128)} custom-call(f32[136,128]{1,0:T(8,128)S(1)} %get-tuple-element.15.e0, f32[136,128]{1,0:T(8,128)S(1)} %collective-permute-done.e1, f32[136,128]{1,0:T(8,128)S(1)} %collective-permute-done.1.e2, f32[136,128]{1,0:T(8,128)S(1)} %collective-permute-done.2.e3), custom_call_target="tpu_custom_call" | custom-call | tf_op jit(solution)/shard_map/route/pallas_call | solution.py:442
  19.7 7.6 %all-to-all-start = ((f32[8,128,128]{2,1,0:T(8,128)}), f32[8,128,128]{2,1,0:T(8,128)S(1)}, u32[]{:S(2)}, u32[]{:S(2)}) async-start(f32[8,128,128]{2,1,0:T(8,128)} %route.1), calls=%async_computation | async-start | bytes 1048576 | tf_op jit(solution)/shard_map/all_to_all | solution.py:446
  27.5 0.5 copy-done.6
  28.0 6.3 %collective-permute-start.5 = (s32[1,1,900]{2,1,0:T(1,128)S(1)}, s32[1,1,900]{2,1,0:T(1,128)S(1)}, u32[]{:S(2)}, u32[]{:S(2)}) collective-permute-start(s32[1,1,900]{2,1,0:T(1,128)S(1)} %copy-done.6), channel_id=1, source_target_pairs={{0,128},{32,160},{64,192},{96,224},{128,0},{160,32},{192,64},{224,... | collective-permute-start | bytes 10808 | tf_op jit(solution)/shard_map/ppermute | solution.py:394
  34.3 1.5 %collective-permute-start.4 = (s32[1,1,900]{2,1,0:T(1,128)S(1)}, s32[1,1,900]{2,1,0:T(1,128)S(1)}, u32[]{:S(2)}, u32[]{:S(2)}) collective-permute-start(s32[1,1,900]{2,1,0:T(1,128)S(1)} %copy-done.6), channel_id=1, source_target_pairs={{0,64},{32,96},{64,128},{96,160},{128,192},{160,224},{192,0},{224,... | collective-permute-start | bytes 10808 | tf_op jit(solution)/shard_map/ppermute | solution.py:394
  35.8 2.7 %collective-permute-start.6 = (s32[1,1,900]{2,1,0:T(1,128)S(1)}, s32[1,1,900]{2,1,0:T(1,128)S(1)}, u32[]{:S(2)}, u32[]{:S(2)}) collective-permute-start(s32[1,1,900]{2,1,0:T(1,128)S(1)} %copy-done.6), channel_id=1, source_target_pairs={{0,192},{32,224},{64,0},{96,32},{128,64},{160,96},{192,128},{224,1... | collective-permute-start | bytes 10808 | tf_op jit(solution)/shard_map/ppermute | solution.py:394
  38.4 1.6 %collective-permute-done.4.q1 = s32[1,1,900]{2,1,0:T(1,128)S(1)} collective-permute-done((s32[1,1,900]{2,1,0:T(1,128)S(1)}, s32[1,1,900]{2,1,0:T(1,128)S(1)}, u32[]{:S(2)}, u32[]{:S(2)}) %collective-permute-start.4) | collective-permute-done | bytes 3632 | tf_op jit(solution)/shard_map/ppermute | solution.py:394
  40.0 0.3 collective-permute-done.6.q3
  40.3 2.7 %lookup.1 = (f32[24,128]{1,0:T(8,128)S(1)}, f32[24,128]{1,0:T(8,128)S(1)}, f32[24,128]{1,0:T(8,128)S(1)}, f32[24,128]{1,0:T(8,128)S(1)}) custom-call(f32[384,128]{1,0:T(8,128)S(1)} %tables.1.own_ref, f32[384,128]{1,0:T(8,128)S(1)} %collective-permute-done.3.mate_ref, s32[1,1,900]{2,1,0:T(1,128)S(1)} %copy-done.6, ...), custom_call_target="tpu_custom_call" | custom-call | tf_op jit(solution)/shard_map/lookup/pallas_call | solution.py:432
  43.0 3.9 %collective-permute-start.7 = (f32[24,128]{1,0:T(8,128)S(1)}, f32[24,128]{1,0:T(8,128)S(1)}, u32[]{:S(2)}, u32[]{:S(2)}) collective-permute-start(f32[24,128]{1,0:T(8,128)S(1)} %get-tuple-element.23), channel_id=1, source_target_pairs={{0,192},{32,224},{64,0},{96,32},{128,64},{160,96},{192,128},{224,1... | collective-permute-start | bytes 36872 | tf_op jit(solution)/shard_map/ppermute | solution.py:394
  46.9 0.9 %collective-permute-start.8 = (f32[24,128]{1,0:T(8,128)S(1)}, f32[24,128]{1,0:T(8,128)S(1)}, u32[]{:S(2)}, u32[]{:S(2)}) collective-permute-start(f32[24,128]{1,0:T(8,128)S(1)} %get-tuple-element.24), channel_id=1, source_target_pairs={{0,128},{32,160},{64,192},{96,224},{128,0},{160,32},{192,64},{224,... | collective-permute-start | bytes 36872 | tf_op jit(solution)/shard_map/ppermute | solution.py:394
  47.8 1.6 %collective-permute-start.9 = (f32[24,128]{1,0:T(8,128)S(1)}, f32[24,128]{1,0:T(8,128)S(1)}, u32[]{:S(2)}, u32[]{:S(2)}) collective-permute-start(f32[24,128]{1,0:T(8,128)S(1)} %get-tuple-element.25), channel_id=1, source_target_pairs={{0,64},{32,96},{64,128},{96,160},{128,192},{160,224},{192,0},{224,... | collective-permute-start | bytes 36872 | tf_op jit(solution)/shard_map/ppermute | solution.py:394
  49.4 5.2 %collective-permute-done.8.r2 = f32[24,128]{1,0:T(8,128)S(1)} collective-permute-done((f32[24,128]{1,0:T(8,128)S(1)}, f32[24,128]{1,0:T(8,128)S(1)}, u32[]{:S(2)}, u32[]{:S(2)}) %collective-permute-start.8) | collective-permute-done | bytes 12320 | tf_op jit(solution)/shard_map/ppermute | solution.py:394
  54.6 2.1 %finish.1 = (f32[2,64,900]{2,1,0:T(8,128)}, f32[2,64,900]{2,1,0:T(8,128)}) custom-call(f32[8,128,128]{2,1,0:T(8,128)S(1)} %all-to-all-done.edge_ref, f32[2,512,128]{2,1,0:T(8,128)S(1)} %get-tuple-element.16.rhs_ref, f32[2,512,128]{2,1,0:T(8,128)S(1)} %get-tuple-element.17.back_ref, f32[192,128]{1,0:T(8,128)S(1)} %get-tuple-element.18.rim_ref, ...), custom_call_target="tpu_custom_call" | custom-call | tf_op jit(solution)/shard_map/finish/pallas_call | solution.py:448
  (22 shorter events, 0.4 us)
Async XLA Ops:
  0.6 1.2 %copy-start = (f32[1,1,2,64,900]{4,3,2,1,0:T(8,128)S(1)}, f32[1,1,2,64,900]{4,3,2,1,0:T(8,128)}, u32[]{:S(2)}) copy-start(f32[1,1,2,64,900]{4,3,2,1,0:T(8,128)} %param.10) | copy-start | bytes 1382404
  1.7 0.7 %copy-start.4 = (s32[1,1,900]{2,1,0:T(1,128)S(1)}, s32[1,1,900]{2,1,0:T(1,128)}, u32[]{:S(2)}) copy-start(s32[1,1,900]{2,1,0:T(1,128)} %param.15) | copy-start | bytes 10804
  1.7 0.7 %copy-start.7 = (s32[1,1,4]{2,1,0:T(1,128)S(1)}, s32[1,1,4]{2,1,0:T(1,128)}, u32[]{:S(2)}) copy-start(s32[1,1,4]{2,1,0:T(1,128)} %param.18) | copy-start | bytes 52
  1.7 0.7 %copy-start.8 = (s32[1,1,4]{2,1,0:T(1,128)S(1)}, s32[1,1,4]{2,1,0:T(1,128)}, u32[]{:S(2)}) copy-start(s32[1,1,4]{2,1,0:T(1,128)} %param.19) | copy-start | bytes 52
  2.4 1.0 %copy-start.1 = (f32[1,1,2,64,900]{4,3,2,1,0:T(8,128)S(1)}, f32[1,1,2,64,900]{4,3,2,1,0:T(8,128)}, u32[]{:S(2)}) copy-start(f32[1,1,2,64,900]{4,3,2,1,0:T(8,128)} %param.11) | copy-start | bytes 1382404
  3.5 1.0 %copy-start.2 = (f32[1,1,2,64,900]{4,3,2,1,0:T(8,128)S(1)}, f32[1,1,2,64,900]{4,3,2,1,0:T(8,128)}, u32[]{:S(2)}) copy-start(f32[1,1,2,64,900]{4,3,2,1,0:T(8,128)} %param.13) | copy-start | bytes 1382404
  11.1 5.4 %collective-permute-start.2 = (f32[136,128]{1,0:T(8,128)S(1)}, f32[136,128]{1,0:T(8,128)S(1)}, u32[]{:S(2)}, u32[]{:S(2)}) collective-permute-start(f32[136,128]{1,0:T(8,128)S(1)} %get-tuple-element.15.e0), channel_id=1, source_target_pairs={{0,3},{1,2},{2,1},{3,0},{4,7},{5,6},{6,5},{7,4},{8,11},{9,10},{10,... | collective-permute-start | bytes 208904 | tf_op jit(solution)/shard_map/ppermute | solution.py:429
  13.3 4.4 %collective-permute-start.1 = (f32[136,128]{1,0:T(8,128)S(1)}, f32[136,128]{1,0:T(8,128)S(1)}, u32[]{:S(2)}, u32[]{:S(2)}) collective-permute-start(f32[136,128]{1,0:T(8,128)S(1)} %get-tuple-element.15.e0), channel_id=1, source_target_pairs={{0,2},{1,3},{2,0},{3,1},{4,6},{5,7},{6,4},{7,5},{8,10},{9,11},{10,... | collective-permute-start | bytes 208904 | tf_op jit(solution)/shard_map/ppermute | solution.py:429
  14.5 4.3 %collective-permute-start = (f32[136,128]{1,0:T(8,128)S(1)}, f32[136,128]{1,0:T(8,128)S(1)}, u32[]{:S(2)}, u32[]{:S(2)}) collective-permute-start(f32[136,128]{1,0:T(8,128)S(1)} %get-tuple-element.15.e0), channel_id=1, source_target_pairs={{0,1},{1,0},{2,3},{3,2},{4,5},{5,4},{6,7},{7,6},{8,9},{9,8},{10,11... | collective-permute-start | bytes 208904 | tf_op jit(solution)/shard_map/ppermute | solution.py:429
  19.7 7.6 %copy-start.3 = (f32[8,16384]{1,0:T(8,128)S(1)}, f32[8,16384]{1,0:T(8,128)}, u32[]{:S(2)}) copy-start(f32[8,16384]{1,0:T(8,128)} %param.16) | copy-start | bytes 1572868
  19.7 34.8 %all-to-all-start = ((f32[8,128,128]{2,1,0:T(8,128)}), f32[8,128,128]{2,1,0:T(8,128)S(1)}, u32[]{:S(2)}, u32[]{:S(2)}) async-start(f32[8,128,128]{2,1,0:T(8,128)} %route.1), calls=%async_computation | async-start | bytes 1048576 | tf_op jit(solution)/shard_map/all_to_all | solution.py:446
  27.3 0.7 %copy-start.6 = (s32[1,1,900]{2,1,0:T(1,128)S(1)}, s32[1,1,900]{2,1,0:T(1,128)}, u32[]{:S(2)}) copy-start(s32[1,1,900]{2,1,0:T(1,128)} %q0.1) | copy-start | bytes 10804
  27.4 12.9 %collective-permute-start.3 = (f32[384,128]{1,0:T(8,128)S(1)}, f32[384,128]{1,0:T(8,128)S(1)}, u32[]{:S(2)}, u32[]{:S(2)}) collective-permute-start(f32[384,128]{1,0:T(8,128)S(1)} %tables.1.own_ref), channel_id=1, source_target_pairs={{0,32},{32,0},{64,96},{96,64},{128,160},{160,128},{192,224},{224,1... | collective-permute-start | bytes 589832 | tf_op jit(solution)/shard_map/ppermute | solution.py:412
  28.0 10.4 %collective-permute-start.5 = (s32[1,1,900]{2,1,0:T(1,128)S(1)}, s32[1,1,900]{2,1,0:T(1,128)S(1)}, u32[]{:S(2)}, u32[]{:S(2)}) collective-permute-start(s32[1,1,900]{2,1,0:T(1,128)S(1)} %copy-done.6), channel_id=1, source_target_pairs={{0,128},{32,160},{64,192},{96,224},{128,0},{160,32},{192,64},{224,... | collective-permute-start | bytes 10808 | tf_op jit(solution)/shard_map/ppermute | solution.py:394
  34.3 5.7 %collective-permute-start.4 = (s32[1,1,900]{2,1,0:T(1,128)S(1)}, s32[1,1,900]{2,1,0:T(1,128)S(1)}, u32[]{:S(2)}, u32[]{:S(2)}) collective-permute-start(s32[1,1,900]{2,1,0:T(1,128)S(1)} %copy-done.6), channel_id=1, source_target_pairs={{0,64},{32,96},{64,128},{96,160},{128,192},{160,224},{192,0},{224,... | collective-permute-start | bytes 10808 | tf_op jit(solution)/shard_map/ppermute | solution.py:394
  35.8 4.5 %collective-permute-start.6 = (s32[1,1,900]{2,1,0:T(1,128)S(1)}, s32[1,1,900]{2,1,0:T(1,128)S(1)}, u32[]{:S(2)}, u32[]{:S(2)}) collective-permute-start(s32[1,1,900]{2,1,0:T(1,128)S(1)} %copy-done.6), channel_id=1, source_target_pairs={{0,192},{32,224},{64,0},{96,32},{128,64},{160,96},{192,128},{224,1... | collective-permute-start | bytes 10808 | tf_op jit(solution)/shard_map/ppermute | solution.py:394
  43.0 6.4 %collective-permute-start.7 = (f32[24,128]{1,0:T(8,128)S(1)}, f32[24,128]{1,0:T(8,128)S(1)}, u32[]{:S(2)}, u32[]{:S(2)}) collective-permute-start(f32[24,128]{1,0:T(8,128)S(1)} %get-tuple-element.23), channel_id=1, source_target_pairs={{0,192},{32,224},{64,0},{96,32},{128,64},{160,96},{192,128},{224,1... | collective-permute-start | bytes 36872 | tf_op jit(solution)/shard_map/ppermute | solution.py:394
  46.9 7.6 %collective-permute-start.8 = (f32[24,128]{1,0:T(8,128)S(1)}, f32[24,128]{1,0:T(8,128)S(1)}, u32[]{:S(2)}, u32[]{:S(2)}) collective-permute-start(f32[24,128]{1,0:T(8,128)S(1)} %get-tuple-element.24), channel_id=1, source_target_pairs={{0,128},{32,160},{64,192},{96,224},{128,0},{160,32},{192,64},{224,... | collective-permute-start | bytes 36872 | tf_op jit(solution)/shard_map/ppermute | solution.py:394
  47.8 6.7 %copy-start.5 = (f32[1,1,2,900]{3,2,1,0:T(2,128)S(1)}, f32[1,1,2,900]{3,2,1,0:T(2,128)}, u32[]{:S(2)}) copy-start(f32[1,1,2,900]{3,2,1,0:T(2,128)} %param.12) | copy-start | bytes 21604
  47.8 6.7 %collective-permute-start.9 = (f32[24,128]{1,0:T(8,128)S(1)}, f32[24,128]{1,0:T(8,128)S(1)}, u32[]{:S(2)}, u32[]{:S(2)}) collective-permute-start(f32[24,128]{1,0:T(8,128)S(1)} %get-tuple-element.25), channel_id=1, source_target_pairs={{0,64},{32,96},{64,128},{96,160},{128,192},{160,224},{192,0},{224,... | collective-permute-start | bytes 36872 | tf_op jit(solution)/shard_map/ppermute | solution.py:394

commit v2 on v1

v2 whole, which is shorter than its diff:
```python
import jax
import jax.numpy as jnp
from jax import lax
from jax.experimental import pallas as pl
from jax.experimental.pallas import tpu as pltpu
from jax.sharding import PartitionSpec as P

SIDE = 30
Z = 64
CELLS = SIDE * SIDE
WIDE = 1024
CHUNKS = WIDE // 128
GROUPS = Z // 8
D = 0.2
CENTRE = 1.0 - 4.0 * D
F32 = jnp.float32
SOLVE_LIMIT = 54 * 1024 * 1024
VMEM_LIMIT = 8 * 1024 * 1024


def lanes(rows, width=WIDE):
    return lax.broadcasted_iota(jnp.int32, (rows, width), 1)


def split(row):
    return [row[:, 128 * c : 128 * c + 128] for c in range(CHUNKS)]


def roll(value, shift):
    return pltpu.roll(value, shift % value.shape[-1], value.ndim - 1)


def grid_masks(rows=1):
    cell = lanes(rows)
    y = lax.shift_right_logical(cell * 2185, 16)
    x = cell - y * SIDE
    return x == 0, x == SIDE - 1, y == 0, y == SIDE - 1


def mirrored(value):
    lane = lanes(value.shape[0], 128)
    back = jnp.bitwise_and(131 - lane, 127)
    turned = [jnp.take_along_axis(part, back, axis=1) for part in split(value)]
    return jnp.concatenate(
        [
            jnp.where(lane < 4, turned[7 - c], turned[max(6 - c, 0)])
            for c in range(CHUNKS)
        ],
        axis=1,
    )


def pieces_of(ref, *at):
    tail = ref[(*at, slice(WIDE - 128, CELLS))]
    fill = jnp.zeros(tail.shape[:-1] + (WIDE - CELLS,), tail.dtype)
    full = [ref[(*at, slice(128 * c, 128 * c + 128))] for c in range(CHUNKS - 1)]
    return full + [jnp.concatenate([tail, fill], axis=-1)]


def put_piece(ref, t, rows, c, value):
    if c < CHUNKS - 1:
        ref[t, rows, 128 * c : 128 * c + 128] = value
    else:
        ref[t, rows, 128 * c : CELLS] = value[:, 0 : CELLS - 128 * c]


def wide(ref, *at):
    return jnp.concatenate(pieces_of(ref, *at), axis=-1)


def make_table(forcing_ref, table_ref):
    wu, wv, ta, qa, pr, ro, ps, ic = [
        forcing_ref[pl.ds(field, 128, stride=8), :] for field in range(8)
    ]
    speed = jnp.sqrt(wu * wu + wv * wv + 1.0)
    carrier = jnp.exp(0.3 * (ps - ta)) * speed / (1.0 + jnp.exp(ic))
    table_ref[0:128, :] = carrier
    table_ref[128:256, :] = carrier * jnp.exp(-0.2 * ps)
    table_ref[256:384, :] = 0.5 * carrier * qa + pr + ro


def lookup_kernel(own_ref, mate_ref, q0, q1, q2, q3, a0, a1, a2, a3, pieces):
    band = lax.axis_index("region")
    for number, ref in enumerate((own_ref, mate_ref)):
        value = ref[...]
        coarse = value.astype(jnp.bfloat16)
        pieces[384 * number : 384 * number + 384, 0:128] = coarse
        pieces[384 * number : 384 * number + 384, 128:256] = (
            value - coarse.astype(F32)
        ).astype(jnp.bfloat16)
    base_own = band * 128
    base_mate = (band + 1 - 2 * lax.rem(band, 2)) * 128
    low = jnp.bitwise_and(lax.broadcasted_iota(jnp.int32, (256, 256), 0), 127)
    high = lax.broadcasted_iota(jnp.int32, (128, 256), 0)
    for q_ref, a_ref in ((q0, a0), (q1, a1), (q2, a2), (q3, a3)):
        points = pieces_of(q_ref, slice(0, 1))
        for part in range(4):
            point = jnp.concatenate(points[2 * part : 2 * part + 2], axis=1)
            onehot = (low == jnp.bitwise_and(point, 127)).astype(jnp.bfloat16)
            found = jnp.dot(pieces[...], onehot, preferred_element_type=F32)
            row = lax.shift_right_logical(point, 7)
            here = high == row - base_own
            there = high == row - base_mate
            for field in range(3):
                picked = jnp.where(here, found[128 * field : 128 * field + 128], 0.0)
                picked = picked + jnp.where(
                    there, found[384 + 128 * field : 512 + 128 * field], 0.0
                )
                total = jnp.sum(picked, axis=0, keepdims=True)
                at = 8 * field + 2 * part
                a_ref[at : at + 1, :] = total[:, 0:128]
                a_ref[at + 1 : at + 2, :] = total[:, 128:256]


def solve_kernel(
    partner_ref, flip_ref, adj_hbm, kap_hbm, depth_hbm, vel_hbm, tan_hbm, forcing_hbm,
    edge_ref, depth_ref, table_ref, solved_hbm, peak_ref, link_ref,
    coup, given, part, solved, adj_ref, kap_ref, forcing_ref, vel_ref, tan_ref, done,
):
    copies = [
        pltpu.make_async_copy(source, target, done.at[number])
        for number, (source, target) in enumerate(
            (
                (kap_hbm, kap_ref),
                (depth_hbm, depth_ref),
                (adj_hbm, adj_ref),
                (forcing_hbm, forcing_ref),
                (vel_hbm, vel_ref),
                (tan_hbm, tan_ref),
            )
        )
    ]
    for copy in copies:
        copy.start()
    copies[0].wait()
    copies[1].wait()
    depths = pieces_of(depth_ref, slice(0, 1))
    for level in range(Z - 1):
        for c, piece in enumerate(pieces_of(kap_ref, level, slice(0, 1))):
            coup[8 * level + c : 8 * level + c + 1, :] = piece
    coup[8 * Z - 8 :, :] = jnp.zeros((8, 128), F32)
    for c, piece in enumerate(depths):
        peak_ref[c : c + 1, :] = piece.astype(F32)
    columns = peak_ref[0:8, :].astype(jnp.int32)

    copies[2].wait()

    def relayout(i, carry):
        rows = pl.ds(pl.multiple_of(8 * i, 8), 8)
        at = pl.multiple_of(64 * i, 64)
        for t in range(2):
            for c, piece in enumerate(pieces_of(adj_ref, t, rows)):
                given[t, pl.ds(at + 8 * c, 8), :] = piece
        return carry

    lax.fori_loop(0, GROUPS, relayout, 0)

    def forward(i, carry):
        e, y_t, y_s, m = carry
        for s in range(8):
            strided = pl.ds(64 * i + s, 8, stride=8)
            packed = pl.ds(pl.multiple_of(64 * i + 8 * s, 8), 8)
            link = jnp.where(8 * i + s + 1 < columns, coup[packed, :], 0.0)
            inv = 1.0 / (e + link)
            y_t = given[0, strided, :] + m * y_t
            y_s = given[1, strided, :] + m * y_s
            m = link * inv
            e = 1.0 + m * e
            link_ref[pl.ds(pl.multiple_of(512 + 64 * i + 8 * s, 8), 8), :] = inv
            link_ref[packed, :] = m
            part[0, packed, :] = y_t * inv
            part[1, packed, :] = y_s * inv
        return e, y_t, y_s, m

    zero = jnp.zeros((8, 128), F32)
    lax.fori_loop(0, GROUPS, forward, (zero + 1.0, zero, zero, zero))

    def backward(n, carry):
        x_t, x_s = carry
        i = GROUPS - 1 - n
        for s in reversed(range(8)):
            strided = pl.ds(64 * i + s, 8, stride=8)
            packed = pl.ds(pl.multiple_of(64 * i + 8 * s, 8), 8)
            m = link_ref[packed, :]
            x_t = part[0, packed, :] + m * x_t
            x_s = part[1, packed, :] + m * x_s
            solved[0, strided, :] = x_t
            solved[1, strided, :] = x_s
        return x_t, x_s

    x_t, x_s = lax.fori_loop(0, GROUPS, backward, (zero, zero))
    peak_ref[0:8, :] = x_t
    peak_ref[8:16, :] = x_s
    keep = pltpu.make_async_copy(solved, solved_hbm, done.at[6])
    keep.start()
    copies[3].wait()
    make_table(forcing_ref, table_ref)
    for copy in copies[4:]:
        copy.wait()

    small = lanes(8, 128)
    south, north = flip_ref[0, 2] == 1, flip_ref[0, 3] == 1
    order = small
    for first, turn in ((0, south), (30, north), (60, south), (90, north)):
        inside = jnp.logical_and(small >= first, small < first + SIDE)
        order = jnp.where(
            jnp.logical_and(inside, turn), 2 * first + SIDE - 1 - small, order
        )
    upper = small >= 102
    level = lax.broadcasted_iota(jnp.int32, (8, 128), 0)

    def pack(i, carry):
        rows = pl.ds(pl.multiple_of(8 * i, 8), 8)
        at = pl.multiple_of(64 * i, 64)
        wet = {c: level + 8 * i < depths[c] for c in (0, 6, 7)}
        speed = pieces_of(vel_ref, 1, rows)
        half = {c: 0.5 * speed[c] for c in (0, 6, 7)}
        for t in range(2):
            value, push = {}, {}
            tracer = pieces_of(tan_ref, t, rows)
            for c in (0, 6, 7):
                value[c] = jnp.where(wet[c], tracer[c], 0.0)
                factor = D + half[c] if c == 0 else D - half[c]
                push[c] = jnp.where(
                    wet[c], factor * solved[t, pl.ds(at + 8 * c, 8), :], 0.0
                )
            edges = jnp.where(small < 30, value[0], 0.0)
            packs = (
                (roll(jnp.where(upper, value[6], value[7]), 56), 30),
                (roll(push[0], 60), 60),
                (roll(jnp.where(upper, push[6], push[7]), 116), 90),
            )
            for piece, first in packs:
                inside = jnp.logical_and(small >= first, small < first + SIDE)
                edges = jnp.where(inside, piece, edges)
            edges = jnp.take_along_axis(edges, order, axis=1)
            edge_ref[pl.ds(pl.multiple_of(64 * t + 8 * i, 8), 8), :] = edges
        return carry

    lax.fori_loop(0, GROUPS, pack, 0, unroll=4)
    second = jnp.logical_or(small < 30, jnp.logical_and(small >= 60, small < 90))
    target = jnp.where(
        second,
        lax.shift_right_logical(partner_ref[0, 2], 2),
        lax.shift_right_logical(partner_ref[0, 3], 2),
    )
    edge_ref[128:136, :] = jnp.where(small < 120, target, -1).astype(F32)
    keep.wait()


def stencil_kernel(
    flip_ref, tan_ref, vel_ref, depth_ref, base_ref, solved, rhs_ref, back_ref, rim_ref,
):
    depth = wide(depth_ref, slice(0, 1))
    sub = lax.broadcasted_iota(jnp.int32, (8, WIDE), 0)
    x0, x29, y0, y29 = grid_masks(8)
    ends = jnp.logical_or(x29, lanes(8) == WIDE - 1)
    turned = jnp.full((8, WIDE), flip_ref[0, 0] == 1)
    turned_x0 = jnp.logical_and(turned, x0)
    turned_x29 = jnp.logical_and(turned, x29)
    small = lanes(8, 128)

    def stencil(i, carry):
        rows = pl.ds(pl.multiple_of(8 * i, 8), 8)
        at = pl.multiple_of(64 * i, 64)
        wet = sub + 8 * i < depth
        half_x, half_y = 0.5 * wide(vel_ref, 0, rows), 0.5 * wide(vel_ref, 1, rows)
        to_e, to_w, to_n, to_s = D - half_x, D + half_x, D - half_y, D + half_y
        for t in range(2):
            value = jnp.where(wet, wide(tan_ref, t, rows), 0.0)
            image = mirrored(value)
            above, below = roll(value, -SIDE), roll(value, SIDE)
            east = roll(jnp.where(x0, below, value), -1)
            west = roll(jnp.where(ends, above, value), 1)
            east = jnp.where(turned_x29, image, east)
            west = jnp.where(turned_x0, image, west)
            mixed = CENTRE * value + to_e * east + to_w * west
            mixed = mixed + to_n * jnp.where(y29, 0.0, above)
            mixed = mixed + to_s * jnp.where(y0, 0.0, below)
            mixed = jnp.where(wet, mixed, 0.0)
            for c, piece in enumerate(split(mixed)):
                rhs_ref[t, pl.ds(at + 8 * c, 8), :] = piece

            answer = jnp.concatenate(
                [solved[t, pl.ds(at + 8 * c, 8), :] for c in range(CHUNKS)], axis=1
            )
            answer = jnp.where(wet, answer, 0.0)
            push_e, push_w = to_e * answer, to_w * answer
            image = mirrored(jnp.where(x29, push_e, push_w))
            moved_e, moved_w = roll(push_e, 1), roll(push_w, -1)
            straight_e = jnp.where(turned_x0, image, jnp.where(x0, 0.0, moved_e))
            straight_w = jnp.where(turned_x29, image, jnp.where(x29, 0.0, moved_w))
            cross_e = jnp.where(x0, jnp.where(turned, 0.0, moved_e), 0.0)
            cross_w = jnp.where(ends, jnp.where(turned, 0.0, moved_w), 0.0)
            inner = CENTRE * answer + straight_e + straight_w
            inner = inner + roll(to_n * answer + cross_w, SIDE)
            inner = inner + roll(to_s * answer + cross_e, -SIDE)
            inner = jnp.where(wet, inner, 0.0)
            for c, piece in enumerate(split(inner)):
                put_piece(back_ref, t, rows, c, piece)
        wet, to_n, to_s = split(wet), split(to_n), split(to_s)
        rim = (
            jnp.where(jnp.logical_and(wet[0], small < SIDE), to_s[0], 0.0),
            jnp.where(jnp.logical_and(wet[6], small >= 102), to_n[6], 0.0),
            jnp.where(jnp.logical_and(wet[7], small < 4), to_n[7], 0.0),
        )
        for number, piece in enumerate(rim):
            rim_ref[pl.ds(pl.multiple_of(64 * number + 8 * i, 8), 8), :] = piece
        return carry

    lax.fori_loop(0, GROUPS, stencil, 0)
    wet = 0 < depth
    for t in range(2):
        first = wide(tan_ref, t, slice(0, 1))
        for c, piece in enumerate(split(jnp.where(wet, first, 0.0))):
            rim_ref[192 + 8 * t + c : 193 + 8 * t + c, :] = piece
        for c, piece in enumerate(pieces_of(base_ref, slice(t, t + 1))):
            rim_ref[208 + 8 * t + c : 209 + 8 * t + c, :] = piece
    for c, piece in enumerate(split(depth)):
        rim_ref[224 + c : 225 + c, :] = piece.astype(F32)


def route_kernel(e0, e1, e2, e3, out_ref):
    mine = lax.shift_right_logical(lax.axis_index("tile"), 3)
    sources = (e0, e1, e2, e3)
    goals = [ref[128:129, :].astype(jnp.int32) for ref in sources]
    for b in range(8):
        total = jnp.zeros((128, 128), F32)
        for goal, ref in zip(goals, sources):
            total = jnp.where(goal == 8 * mine + b, ref[0:128, :], total)
        out_ref[b] = total


def finish_kernel(
    edge_ref, rhs_ref, back_hbm, rim_ref, peak_ref, link_ref,
    r0, r1, r2, r3, depth_ref, next_hbm, prev_hbm,
    right, part, solved, next_ref, prev_ref, done,
):
    fetch = pltpu.make_async_copy(back_hbm, prev_ref, done.at[2])
    fetch.start()
    depth = wide(depth_ref, slice(0, 1))
    carrier, scaled, loss = [
        sum(ref[8 * f : 8 * f + 8, :] for ref in (r0, r1, r2, r3)) for f in range(3)
    ]
    moist = scaled * jnp.exp(0.5 * rim_ref[208:216, :])
    wet = rim_ref[224:232, :] > 0.0
    heat_self = jnp.where(wet, -(0.5 * carrier + 0.25 * moist), 0.0)
    salt_heat = jnp.where(wet, 0.25 * rim_ref[216:224, :] * moist, 0.0)
    salt_self = jnp.where(wet, 0.5 * moist - loss, 0.0)
    tan_t, tan_s = rim_ref[192:200, :], rim_ref[200:208, :]
    adj_t, adj_s = peak_ref[0:8, :], peak_ref[8:16, :]

    small = lanes(8, 128)
    sub = lax.broadcasted_iota(jnp.int32, (8, WIDE), 0)

    def rims(i, carry):
        rows = pl.ds(pl.multiple_of(8 * i, 8), 8)
        at = pl.multiple_of(64 * i, 64)
        wet = split(sub + 8 * i < depth)
        rim = [rim_ref[pl.ds(pl.multiple_of(64 * n + 8 * i, 8), 8), :] for n in range(3)]
        for t in range(2):
            where = pl.ds(pl.multiple_of(64 * t + 8 * i, 8), 8)
            edge = edge_ref[0, where, :]
            for b in range(1, 8):
                edge = edge + edge_ref[b, where, :]
            north = roll(edge, 72)
            from_s, from_n = roll(edge, 68), roll(edge, 12)
            for c in range(CHUNKS):
                put = pl.ds(at + 8 * c, 8)
                value = rhs_ref[t, put, :]
                if c == 0:
                    value = value + rim[0] * edge
                elif c >= 6:
                    value = value + rim[c - 5] * north
                right[t, put, :] = value
            insides = (
                (0, jnp.logical_and(wet[0], small < SIDE), from_s),
                (6, jnp.logical_and(wet[6], small >= 102), from_n),
                (7, jnp.logical_and(wet[7], small < 4), from_n),
            )
            for c, inside, piece in insides:
                spot = slice(128 * c, min(128 * c + 128, CELLS))
                piece = jnp.where(inside, piece, 0.0)[:, 0 : spot.stop - spot.start]
                prev_ref[t, rows, spot] = prev_ref[t, rows, spot] + piece
        return carry

    fetch.wait()
    lax.fori_loop(0, GROUPS, rims, 0)
    zero = jnp.zeros((8, 128), F32)
    first = pl.ds(0, 8, stride=8)
    right[0, first, :] = right[0, first, :] + heat_self * tan_t
    right[1, first, :] = right[1, first, :] + salt_heat * tan_t + salt_self * tan_s
    adds = (heat_self * adj_t + salt_heat * adj_s, salt_self * adj_s)
    for t, add in enumerate(adds):
        for c in range(CHUNKS):
            spot = slice(128 * c, min(128 * c + 128, CELLS))
            more = add[c : c + 1, 0 : spot.stop - spot.start]
            prev_ref[t, 0:1, spot] = prev_ref[t, 0:1, spot] + more
    copy_prev = pltpu.make_async_copy(prev_ref, prev_hbm, done.at[0])
    copy_prev.start()

    def forward(i, carry):
        y_t, y_s, m = carry
        for s in range(8):
            strided = pl.ds(64 * i + s, 8, stride=8)
            packed = pl.ds(pl.multiple_of(64 * i + 8 * s, 8), 8)
            y_t = right[0, strided, :] + m * y_t
            y_s = right[1, strided, :] + m * y_s
            m = link_ref[packed, :]
            inv = link_ref[pl.ds(pl.multiple_of(512 + 64 * i + 8 * s, 8), 8), :]
            part[0, packed, :] = y_t * inv
            part[1, packed, :] = y_s * inv
        return y_t, y_s, m

    lax.fori_loop(0, GROUPS, forward, (zero, zero, zero))

    def backward(n, carry):
        x_t, x_s = carry
        i = GROUPS - 1 - n
        for s in reversed(range(8)):
            strided = pl.ds(64 * i + s, 8, stride=8)
            packed = pl.ds(pl.multiple_of(64 * i + 8 * s, 8), 8)
            m = link_ref[packed, :]
            x_t = part[0, packed, :] + m * x_t
            x_s = part[1, packed, :] + m * x_s
            solved[0, strided, :] = x_t
            solved[1, strided, :] = x_s
        return x_t, x_s

    lax.fori_loop(0, GROUPS, backward, (zero, zero))

    def write(i, carry):
        rows = pl.ds(pl.multiple_of(8 * i, 8), 8)
        at = pl.multiple_of(64 * i, 64)
        for t in range(2):
            for c in range(CHUNKS):
                put_piece(next_ref, t, rows, c, solved[t, pl.ds(at + 8 * c, 8), :])
        return carry

    lax.fori_loop(0, GROUPS, write, 0)
    copy_next = pltpu.make_async_copy(next_ref, next_hbm, done.at[1])
    copy_next.start()
    copy_next.wait()
    copy_prev.wait()


def call(kernel, name, micros, ins, outs, scratch=(), limit=VMEM_LIMIT):
    places = {"S": pltpu.SMEM, "V": pltpu.VMEM, "H": pltpu.HBM}
    shapes = [
        out if isinstance(out, jax.ShapeDtypeStruct) else jax.ShapeDtypeStruct(out, F32)
        for _, out in outs
    ]
    return pl.pallas_call(
        kernel,
        in_specs=[pl.BlockSpec(memory_space=places[place]) for place in ins],
        out_specs=[pl.BlockSpec(memory_space=places[place]) for place, _ in outs],
        out_shape=shapes,
        scratch_shapes=list(scratch),
        compiler_params=pltpu.CompilerParams(vmem_limit_bytes=limit),
        cost_estimate=pl.CostEstimate(
            flops=0, bytes_accessed=int(3.69e6 * micros), transcendentals=0
        ),
        name=name,
    )


def swap(value, axis, size, bit):
    return lax.ppermute(value, axis, [(i, i ^ bit) for i in range(size)])


def hops():
    ways = ([], [], [])
    for h in range(4):
        for low in range(2):
            step = 2 * low - 1
            targets = (((h + step) % 4, 1 - low), ((h - step) % 4, low), ((h + 2) % 4, 1 - low))
            for way, (there, low_there) in zip(ways, targets):
                for core in range(2):
                    for column in range(16):
                        source = (2 * h + core) * 32 + 2 * column + low
                        target = (2 * there + core) * 32 + 2 * column + low_there
                        way.append((source, target))
    return ways


def shards(
    tangent, adjoint, base, velocity, kappa, depth_levels, forcing, forcing_point, partner_edge,
    edge_flip,
):
    tangent, adjoint, velocity = tangent[0, 0], adjoint[0, 0], velocity[0, 0]
    base, kappa, depth = base[0, 0], kappa.reshape(Z - 1, 1, CELLS), depth_levels[0]
    mine, partner, flip = forcing_point[0], partner_edge[0], edge_flip[0]
    blocked = (2, 8 * Z, 128)
    flat = (8 * Z, 128)
    natural = (2, Z, CELLS)
    answer = (24, 128)
    line = jax.ShapeDtypeStruct((1, CELLS), jnp.int32)
    both = ("region", "tile")

    asked = [lax.ppermute(mine, both, way) for way in hops()]
    banded = forcing.reshape(8, 128, 128).transpose(1, 0, 2).reshape(1024, 128)
    edges, depth, table, solved, peak, link = call(
        solve_kernel,
        "solve",
        4.0,
        "SSHHHHHH",
        [("V", (136, 128)), ("V", line), ("V", (384, 128))]
        + [("H", blocked), ("V", (16, 128)), ("V", (16 * Z, 128))],
        [
            pltpu.VMEM(flat, F32),
            pltpu.VMEM(blocked, F32),
            pltpu.VMEM(blocked, F32),
            pltpu.VMEM(blocked, F32),
            pltpu.VMEM(natural, F32),
            pltpu.VMEM((Z - 1, 1, CELLS), F32),
            pltpu.VMEM((1024, 128), F32),
            pltpu.VMEM(natural, F32),
            pltpu.VMEM(natural, F32),
            pltpu.SemaphoreType.DMA((7,)),
        ],
        limit=SOLVE_LIMIT,
    )(partner, flip, adjoint, kappa, depth, velocity, tangent, banded)
    table, edges, asked = lax.optimization_barrier((table, edges, asked))
    mate = swap(table, "region", 8, 1)
    edge = [edges] + [swap(edges, "tile", 32, k) for k in (8, 16, 24)]

    table, edges = lax.optimization_barrier((table, edges))
    answers = call(
        lookup_kernel,
        "lookup",
        2.7,
        "V" * 6,
        [("V", answer)] * 4,
        [pltpu.VMEM((768, 256), jnp.bfloat16)],
    )(table, mate, mine, *asked)
    replies = [answers[0]] + [
        lax.ppermute(value, both, [(target, source) for source, target in way])
        for value, way in zip(answers[1:], hops())
    ]

    edge[0], first = lax.optimization_barrier((edge[0], answers[0]))
    (slots,) = call(route_kernel, "route", 0.9, "VVVV", [("V", (8, 128, 128))])(*edge)
    groups = [[8 * a + b for b in range(8)] for a in range(4)]
    arrived = lax.all_to_all(slots, "tile", 0, 0, axis_index_groups=groups, tiled=True)

    rhs, back, rim = call(
        stencil_kernel,
        "stencil",
        3.0,
        "SVVVVV",
        [("V", blocked), ("V", natural), ("V", (232, 128))],
    )(flip, tangent, velocity, depth, base, solved)

    following, previous = call(
        finish_kernel,
        "finish",
        2.1,
        "VVHVVVVVVVV",
        [("H", natural), ("H", natural)],
        [
            pltpu.VMEM(blocked, F32),
            pltpu.VMEM(blocked, F32),
            pltpu.VMEM(blocked, F32),
            pltpu.VMEM(natural, F32),
            pltpu.VMEM(natural, F32),
            pltpu.SemaphoreType.DMA((3,)),
        ],
    )(arrived, rhs, back, rim, peak, link, *replies, depth)
    return following[None, None], previous[None, None]


def solution(mesh):
    fields = P("region", "tile", None, None, None)
    rows = P("region", "tile", None, None)
    single = P("region", "tile", None)
    in_specs = (fields, fields, rows, fields, rows, single, P(None, "region"), single, single, single)
    return jax.shard_map(
        shards, mesh=mesh, in_specs=in_specs, out_specs=(fields, fields), check_vma=False
    )
```

time: 57 us -> 44 us (0.77)
  waiting for transfers between devices: 11.2 us -> 3.05 us
  starting transfers between devices: 28.1 us -> 23.6 us
  local copies, waits for them, and re-layouts: 4.32 us -> 2.63 us
  Pallas kernels: 12.4 us -> 13.6 us
    ppermute x10, waiting for transfers between devices: 11.2 us -> 3.04 us  [the longest x4 1.98 us: swap(): return lax.ppermute(value, axis, [(i, i ^ bit) for i in range(size)])]
    all_to_all x1, starting transfers between devices: 7.56 us -> 4.91 us  [shards(): lax.all_to_all(slots, 'tile', 0, 0, axis_index_groups=groups, tiled=True)]
    ppermute x10, starting transfers between devices: 20.5 us -> 18.7 us  [the longest x3 8.31 us: shards(): asked = [lax.ppermute(mine, both, way) for way in hops()]]
    unnamed x19 -> x22, local copies, waits for them, and re-layouts: 4.32 us -> 2.63 us
    pallas_call x5, Pallas kernels: 12.4 us -> 13.6 us  [the longest x1 4.59 us: shards(): call(solve_kernel, 'solve', 4.0, 'SSHHHHHH', [('V', (136, 128)), ('V', li...]
  transfers between devices with their start and end apart: 11 -> 11, of which waited for: 6 -> 3; matrix products, arithmetic and copies ran while one was open for 0% -> 0% of each run, Pallas kernels for 5% -> 24%
where the time goes in v2:
time: 44 us; the launch traced here: 43.6 us
  starting transfers between devices  23.6 us (54%)
  Pallas kernels  13.6 us (31%)
  waiting for transfers between devices  3.05 us (7%)
  local copies, waits for them, and re-layouts  2.63 us (6%)
  between operations  0.74 us (2%)
    ppermute x3, starting transfers between devices, shards(): asked = [lax.ppermute(mine, both, way) for way in hops()]  8.31 us
    ppermute x3, starting transfers between devices, shards(): lax.ppermute(value, both, [(target, source) for source, target in way])  6.33 us
    all_to_all x1, starting transfers between devices, shards(): lax.all_to_all(slots, 'tile', 0, 0, axis_index_groups=groups, tiled=True)  4.91 us
    pallas_call x1, Pallas kernels, shards(): call(solve_kernel, 'solve', 4.0, 'SSHHHHHH', [('V', (136, 128)), ('V', li...  4.59 us
    ppermute x4, starting transfers between devices, swap(): return lax.ppermute(value, axis, [(i, i ^ bit) for i in range(size)])  4.1 us
    pallas_call x1, Pallas kernels, shards(): call(stencil_kernel, 'stencil', 3.0, 'SVVVVV', [('V', blocked), ('V', nat...  3.33 us
    pallas_call x1, Pallas kernels, shards(): call(lookup_kernel, 'lookup', 2.7, 'V' * 6, [('V', answer)] * 4, [pltpu.V...  2.73 us
    unnamed x22, local copies, waits for them, and re-layouts  2.63 us
  transfers between devices with their start and end apart: 11, of which 3 were waited for; matrix products, arithmetic and copies ran while one was open for 0% of the time, Pallas kernels for 24%

profile of v2, /device:TPU:6, one launch (start us, length us, event | category | flops | bytes accessed | tf_op | source)
XLA Modules:
  0.0 43.6 jit_solution(12037149509644925189)
XLA Ops:
  0.6 6.8 %collective-permute-start.2 = (s32[1,900]{1,0:T(1,128)}, s32[1,900]{1,0:T(1,128)S(1)}, u32[]{:S(2)}, u32[]{:S(2)}) collective-permute-start(s32[1,900]{1,0:T(1,128)} %bitcast.21), channel_id=1, source_target_pairs={{0,129},{2,131},{4,133},{6,135},{8,137},{10,139},{12,141},{14,143}... | collective-permute-start | bytes 10808 | tf_op jit(solution)/shard_map/ppermute | solution.py:500
  7.5 1.5 %collective-permute-start.1 = (s32[1,900]{1,0:T(1,128)}, s32[1,900]{1,0:T(1,128)S(1)}, u32[]{:S(2)}, u32[]{:S(2)}) collective-permute-start(s32[1,900]{1,0:T(1,128)} %bitcast.22), channel_id=1, source_target_pairs={{0,64},{2,66},{4,68},{6,70},{8,72},{10,74},{12,76},{14,78},{16,80}... | collective-permute-start | bytes 10808 | tf_op jit(solution)/shard_map/ppermute | solution.py:500
  8.9 0.0 collective-permute-start
  8.9 4.6 %solve.1 = (f32[136,128]{1,0:T(8,128)}, s32[1,900]{1,0:T(1,128)}, f32[384,128]{1,0:T(8,128)}, f32[2,512,128]{2,1,0:T(8,128)}, f32[16,128]{1,0:T(8,128)}, /*index=5*/f32[1024,128]{1,0:T(8,128)}) custom-call(s32[1,4]{1,0:T(1,128)} %bitcast.31, s32[1,4]{1,0:T(1,128)} %bitcast.25, f32[2,64,900]{2,1,0:T(8,128)} %bitcast.27, f32[63,1,900]{2,1,0:T(1,128)} %bitcast.29, ...), custom_call_target="tpu_custom_call" | custom-call | bytes 14760000 | tf_op jit(solution)/shard_map/solve/pallas_call | solution.py:502
  13.6 0.0 collective-permute-done.1.q2
  13.6 0.4 collective-permute-done.q1
  14.0 0.0 collective-permute-start.3
  14.0 3.0 %collective-permute-start.6 = (f32[136,128]{1,0:T(8,128)}, f32[136,128]{1,0:T(8,128)S(1)}, u32[]{:S(2)}, u32[]{:S(2)}) collective-permute-start(f32[136,128]{1,0:T(8,128)} %get-tuple-element.33.e0), channel_id=1, source_target_pairs={{0,24},{1,25},{2,26},{3,27},{4,28},{5,29},{6,30},{7,31},{8,16},{9,... | collective-permute-start | bytes 208904 | tf_op jit(solution)/shard_map/ppermute | solution.py:468
  17.0 0.6 %collective-permute-start.5 = (f32[136,128]{1,0:T(8,128)}, f32[136,128]{1,0:T(8,128)S(1)}, u32[]{:S(2)}, u32[]{:S(2)}) collective-permute-start(f32[136,128]{1,0:T(8,128)} %get-tuple-element.33.e0), channel_id=1, source_target_pairs={{0,16},{1,17},{2,18},{3,19},{4,20},{5,21},{6,22},{7,23},{8,24},{9,... | collective-permute-start | bytes 208904 | tf_op jit(solution)/shard_map/ppermute | solution.py:468
  17.6 0.5 %collective-permute-start.4 = (f32[136,128]{1,0:T(8,128)}, f32[136,128]{1,0:T(8,128)S(1)}, u32[]{:S(2)}, u32[]{:S(2)}) collective-permute-start(f32[136,128]{1,0:T(8,128)} %get-tuple-element.33.e0), channel_id=1, source_target_pairs={{0,8},{1,9},{2,10},{3,11},{4,12},{5,13},{6,14},{7,15},{8,0},{9,1},... | collective-permute-start | bytes 208904 | tf_op jit(solution)/shard_map/ppermute | solution.py:468
  18.1 0.9 %copy-done.4 = f32[384,128]{1,0:T(8,128)S(1)} copy-done((f32[384,128]{1,0:T(8,128)S(1)}, f32[384,128]{1,0:T(8,128)}, u32[]{:S(2)}) %copy-start.4) | copy-done | bytes 196632
  19.0 2.7 %lookup.1 = (f32[24,128]{1,0:T(8,128)S(1)}, f32[24,128]{1,0:T(8,128)S(1)}, f32[24,128]{1,0:T(8,128)S(1)}, f32[24,128]{1,0:T(8,128)S(1)}) custom-call(f32[384,128]{1,0:T(8,128)S(1)} %copy-done.4, f32[384,128]{1,0:T(8,128)S(1)} %collective-permute-done.3.mate_ref, s32[1,900]{1,0:T(1,128)S(1)} %bitcast.24, s32[1,900]{1,0:T(1,128)S(1)} %collective-permute-done.q1, ...), custom_call_target="tpu_custom_call" | custom-call | bytes 9963000 | tf_op jit(solution)/shard_map/lookup/pallas_call | solution.py:528
  21.7 0.0 collective-permute-done.6.e3
  21.7 2.0 %collective-permute-done.5.e2 = f32[136,128]{1,0:T(8,128)S(1)} collective-permute-done((f32[136,128]{1,0:T(8,128)}, f32[136,128]{1,0:T(8,128)S(1)}, u32[]{:S(2)}, u32[]{:S(2)}) %collective-permute-start.5) | collective-permute-done | bytes 69664 | tf_op jit(solution)/shard_map/ppermute | solution.py:468
  23.7 0.9 %route.1 = f32[8,128,128]{2,1,0:T(8,128)} custom-call(f32[136,128]{1,0:T(8,128)S(1)} %copy-done.5, f32[136,128]{1,0:T(8,128)S(1)} %collective-permute-done.4.e1, f32[136,128]{1,0:T(8,128)S(1)} %collective-permute-done.5.e2, f32[136,128]{1,0:T(8,128)S(1)} %collective-permute-done.6.e3), custom_call_target="tpu_custom_call" | custom-call | bytes 3321000 | tf_op jit(solution)/shard_map/route/pallas_call | solution.py:542
  24.6 4.9 %all-to-all-start = ((f32[8,128,128]{2,1,0:T(8,128)}), f32[8,128,128]{2,1,0:T(8,128)S(1)}, u32[]{:S(2)}, u32[]{:S(2)}) async-start(f32[8,128,128]{2,1,0:T(8,128)} %route.1), calls=%async_computation | async-start | bytes 1048576 | tf_op jit(solution)/shard_map/all_to_all | solution.py:544
  29.5 3.9 %collective-permute-start.7 = (f32[24,128]{1,0:T(8,128)S(1)}, f32[24,128]{1,0:T(8,128)S(1)}, u32[]{:S(2)}, u32[]{:S(2)}) collective-permute-start(f32[24,128]{1,0:T(8,128)S(1)} %get-tuple-element.41), channel_id=1, source_target_pairs={{193,0},{195,2},{197,4},{199,6},{201,8},{203,10},{205,12},{207,14}... | collective-permute-start | bytes 36872 | tf_op jit(solution)/shard_map/ppermute | solution.py:537
  33.4 1.5 %collective-permute-start.8 = (f32[24,128]{1,0:T(8,128)S(1)}, f32[24,128]{1,0:T(8,128)S(1)}, u32[]{:S(2)}, u32[]{:S(2)}) collective-permute-start(f32[24,128]{1,0:T(8,128)S(1)} %get-tuple-element.42), channel_id=1, source_target_pairs={{64,0},{66,2},{68,4},{70,6},{72,8},{74,10},{76,12},{78,14},{80,16}... | collective-permute-start | bytes 36872 | tf_op jit(solution)/shard_map/ppermute | solution.py:537
  34.9 1.0 %collective-permute-start.9 = (f32[24,128]{1,0:T(8,128)S(1)}, f32[24,128]{1,0:T(8,128)S(1)}, u32[]{:S(2)}, u32[]{:S(2)}) collective-permute-start(f32[24,128]{1,0:T(8,128)S(1)} %get-tuple-element.43), channel_id=1, source_target_pairs={{129,0},{131,2},{133,4},{135,6},{137,8},{139,10},{141,12},{143,14}... | collective-permute-start | bytes 36872 | tf_op jit(solution)/shard_map/ppermute | solution.py:537
  35.9 0.6 %copy-done.10 = s32[1,1,4]{2,1,0:T(1,128)S(1)} copy-done((s32[1,1,4]{2,1,0:T(1,128)S(1)}, s32[1,1,4]{2,1,0:T(1,128)}, u32[]{:S(2)}) %copy-start.10) | copy-done | bytes 40
  36.5 1.0 %copy-done.3 = f32[2,512,128]{2,1,0:T(8,128)S(1)} copy-done((f32[2,512,128]{2,1,0:T(8,128)S(1)}, f32[2,512,128]{2,1,0:T(8,128)}, u32[]{:S(2)}) %copy-start.3) | copy-done | bytes 524312
  37.6 3.3 %stencil.1 = (f32[2,512,128]{2,1,0:T(8,128)S(1)}, f32[2,64,900]{2,1,0:T(8,128)S(1)}, f32[232,128]{1,0:T(8,128)S(1)}) custom-call(s32[1,4]{1,0:T(1,128)S(1)} %bitcast.26, f32[2,64,900]{2,1,0:T(8,128)S(1)} %bitcast.19, f32[2,64,900]{2,1,0:T(8,128)S(1)} %bitcast.17, s32[1,900]{1,0:T(1,128)S(1)} %copy-done.6, f32[2,900]{1,0:T(2,128)S(1)} %bitcast.20, ...), custom_call_target="tpu_custom_call" | custom-call | bytes 11070000 | tf_op jit(solution)/shard_map/stencil/pallas_call | solution.py:546
  41.0 0.7 %collective-permute-done.9.r3 = f32[24,128]{1,0:T(8,128)S(1)} collective-permute-done((f32[24,128]{1,0:T(8,128)S(1)}, f32[24,128]{1,0:T(8,128)S(1)}, u32[]{:S(2)}, u32[]{:S(2)}) %collective-permute-start.9) | collective-permute-done | bytes 12320 | tf_op jit(solution)/shard_map/ppermute | solution.py:537
  41.6 2.0 %finish.1 = (f32[2,64,900]{2,1,0:T(8,128)}, f32[2,64,900]{2,1,0:T(8,128)}) custom-call(f32[8,128,128]{2,1,0:T(8,128)S(1)} %all-to-all-done.edge_ref, f32[2,512,128]{2,1,0:T(8,128)S(1)} %get-tuple-element.36.rhs_ref, f32[2,64,900]{2,1,0:T(8,128)S(1)} %get-tuple-element.37.back_hbm, f32[232,128]{1,0:T(8,128)S(1)} %get-tuple-element.38.rim_ref, ...), custom_call_target="tpu_custom_call" | custom-call | bytes 7749000 | tf_op jit(solution)/shard_map/finish/pallas_call | solution.py:554
  (25 shorter events, 0.1 us)
Async XLA Ops:
  0.6 12.9 %collective-permute-start.2 = (s32[1,900]{1,0:T(1,128)}, s32[1,900]{1,0:T(1,128)S(1)}, u32[]{:S(2)}, u32[]{:S(2)}) collective-permute-start(s32[1,900]{1,0:T(1,128)} %bitcast.21), channel_id=1, source_target_pairs={{0,129},{2,131},{4,133},{6,135},{8,137},{10,139},{12,141},{14,143}... | collective-permute-start | bytes 10808 | tf_op jit(solution)/shard_map/ppermute | solution.py:500
  7.5 6.1 %collective-permute-start.1 = (s32[1,900]{1,0:T(1,128)}, s32[1,900]{1,0:T(1,128)S(1)}, u32[]{:S(2)}, u32[]{:S(2)}) collective-permute-start(s32[1,900]{1,0:T(1,128)} %bitcast.22), channel_id=1, source_target_pairs={{0,64},{2,66},{4,68},{6,70},{8,72},{10,74},{12,76},{14,78},{16,80}... | collective-permute-start | bytes 10808 | tf_op jit(solution)/shard_map/ppermute | solution.py:500
  8.9 5.0 %collective-permute-start = (s32[1,900]{1,0:T(1,128)}, s32[1,900]{1,0:T(1,128)S(1)}, u32[]{:S(2)}, u32[]{:S(2)}) collective-permute-start(s32[1,900]{1,0:T(1,128)} %bitcast.23), channel_id=1, source_target_pairs={{0,193},{2,195},{4,197},{6,199},{8,201},{10,203},{12,205},{14,207}... | collective-permute-start | bytes 10808 | tf_op jit(solution)/shard_map/ppermute | solution.py:500
  8.9 9.1 %copy-start.9 = (s32[1,1,900]{2,1,0:T(1,128)S(1)}, s32[1,1,900]{2,1,0:T(1,128)}, u32[]{:S(2)}) copy-start(s32[1,1,900]{2,1,0:T(1,128)} %param.17) | copy-start | bytes 10804
  14.0 4.1 %collective-permute-start.3 = (f32[384,128]{1,0:T(8,128)}, f32[384,128]{1,0:T(8,128)S(1)}, u32[]{:S(2)}, u32[]{:S(2)}) collective-permute-start(f32[384,128]{1,0:T(8,128)} %get-tuple-element.28.own_ref), channel_id=1, source_target_pairs={{0,32},{32,0},{64,96},{96,64},{128,160},{160,128},{192,224},{224,1... | collective-permute-start | bytes 589832 | tf_op jit(solution)/shard_map/ppermute | solution.py:468
  14.0 7.8 %collective-permute-start.6 = (f32[136,128]{1,0:T(8,128)}, f32[136,128]{1,0:T(8,128)S(1)}, u32[]{:S(2)}, u32[]{:S(2)}) collective-permute-start(f32[136,128]{1,0:T(8,128)} %get-tuple-element.33.e0), channel_id=1, source_target_pairs={{0,24},{1,25},{2,26},{3,27},{4,28},{5,29},{6,30},{7,31},{8,16},{9,... | collective-permute-start | bytes 208904 | tf_op jit(solution)/shard_map/ppermute | solution.py:468
  17.0 6.7 %collective-permute-start.5 = (f32[136,128]{1,0:T(8,128)}, f32[136,128]{1,0:T(8,128)S(1)}, u32[]{:S(2)}, u32[]{:S(2)}) collective-permute-start(f32[136,128]{1,0:T(8,128)} %get-tuple-element.33.e0), channel_id=1, source_target_pairs={{0,16},{1,17},{2,18},{3,19},{4,20},{5,21},{6,22},{7,23},{8,24},{9,... | collective-permute-start | bytes 208904 | tf_op jit(solution)/shard_map/ppermute | solution.py:468
  17.6 6.1 %collective-permute-start.4 = (f32[136,128]{1,0:T(8,128)}, f32[136,128]{1,0:T(8,128)S(1)}, u32[]{:S(2)}, u32[]{:S(2)}) collective-permute-start(f32[136,128]{1,0:T(8,128)} %get-tuple-element.33.e0), channel_id=1, source_target_pairs={{0,8},{1,9},{2,10},{3,11},{4,12},{5,13},{6,14},{7,15},{8,0},{9,1},... | collective-permute-start | bytes 208904 | tf_op jit(solution)/shard_map/ppermute | solution.py:468
  18.1 0.9 %copy-start.4 = (f32[384,128]{1,0:T(8,128)S(1)}, f32[384,128]{1,0:T(8,128)}, u32[]{:S(2)}) copy-start(f32[384,128]{1,0:T(8,128)} %get-tuple-element.28.own_ref) | copy-start | bytes 589828
  19.0 4.7 %copy-start.5 = (f32[136,128]{1,0:T(8,128)S(1)}, f32[136,128]{1,0:T(8,128)}, u32[]{:S(2)}) copy-start(f32[136,128]{1,0:T(8,128)} %get-tuple-element.33.e0) | copy-start | bytes 208900
  23.7 12.2 %copy-start.7 = (f32[1,1,2,900]{3,2,1,0:T(2,128)S(1)}, f32[1,1,2,900]{3,2,1,0:T(2,128)}, u32[]{:S(2)}) copy-start(f32[1,1,2,900]{3,2,1,0:T(2,128)} %param.12) | copy-start | bytes 21604
  24.6 11.3 %copy-start = (f32[1,1,2,64,900]{4,3,2,1,0:T(8,128)S(1)}, f32[1,1,2,64,900]{4,3,2,1,0:T(8,128)}, u32[]{:S(2)}) copy-start(f32[1,1,2,64,900]{4,3,2,1,0:T(8,128)} %param.13) | copy-start | bytes 1382404
  24.6 11.3 %copy-start.1 = (f32[1,1,2,64,900]{4,3,2,1,0:T(8,128)S(1)}, f32[1,1,2,64,900]{4,3,2,1,0:T(8,128)}, u32[]{:S(2)}) copy-start(f32[1,1,2,64,900]{4,3,2,1,0:T(8,128)} %param.10) | copy-start | bytes 1382404
  24.6 17.0 %all-to-all-start = ((f32[8,128,128]{2,1,0:T(8,128)}), f32[8,128,128]{2,1,0:T(8,128)S(1)}, u32[]{:S(2)}, u32[]{:S(2)}) async-start(f32[8,128,128]{2,1,0:T(8,128)} %route.1), calls=%async_computation | async-start | bytes 1048576 | tf_op jit(solution)/shard_map/all_to_all | solution.py:544
  29.5 11.4 %collective-permute-start.7 = (f32[24,128]{1,0:T(8,128)S(1)}, f32[24,128]{1,0:T(8,128)S(1)}, u32[]{:S(2)}, u32[]{:S(2)}) collective-permute-start(f32[24,128]{1,0:T(8,128)S(1)} %get-tuple-element.41), channel_id=1, source_target_pairs={{193,0},{195,2},{197,4},{199,6},{201,8},{203,10},{205,12},{207,14}... | collective-permute-start | bytes 36872 | tf_op jit(solution)/shard_map/ppermute | solution.py:537
  33.4 2.5 %copy-start.6 = (s32[1,900]{1,0:T(1,128)S(1)}, s32[1,900]{1,0:T(1,128)}, u32[]{:S(2)}) copy-start(s32[1,900]{1,0:T(1,128)} %get-tuple-element.34.depth_ref) | copy-start | bytes 10804
  33.4 7.5 %collective-permute-start.8 = (f32[24,128]{1,0:T(8,128)S(1)}, f32[24,128]{1,0:T(8,128)S(1)}, u32[]{:S(2)}, u32[]{:S(2)}) collective-permute-start(f32[24,128]{1,0:T(8,128)S(1)} %get-tuple-element.42), channel_id=1, source_target_pairs={{64,0},{66,2},{68,4},{70,6},{72,8},{74,10},{76,12},{78,14},{80,16}... | collective-permute-start | bytes 36872 | tf_op jit(solution)/shard_map/ppermute | solution.py:537
  34.9 6.7 %collective-permute-start.9 = (f32[24,128]{1,0:T(8,128)S(1)}, f32[24,128]{1,0:T(8,128)S(1)}, u32[]{:S(2)}, u32[]{:S(2)}) collective-permute-start(f32[24,128]{1,0:T(8,128)S(1)} %get-tuple-element.43), channel_id=1, source_target_pairs={{129,0},{131,2},{133,4},{135,6},{137,8},{139,10},{141,12},{143,14}... | collective-permute-start | bytes 36872 | tf_op jit(solution)/shard_map/ppermute | solution.py:537
  35.9 0.7 %copy-start.10 = (s32[1,1,4]{2,1,0:T(1,128)S(1)}, s32[1,1,4]{2,1,0:T(1,128)}, u32[]{:S(2)}) copy-start(s32[1,1,4]{2,1,0:T(1,128)} %param.19) | copy-start | bytes 52
  36.5 1.0 %copy-start.3 = (f32[2,512,128]{2,1,0:T(8,128)S(1)}, f32[2,512,128]{2,1,0:T(8,128)}, u32[]{:S(2)}) copy-start(f32[2,512,128]{2,1,0:T(8,128)} %get-tuple-element.35.solved) | copy-start | bytes 1572868
  37.6 4.0 %copy-start.2 = (f32[1024,128]{1,0:T(8,128)S(1)}, f32[1024,128]{1,0:T(8,128)}, u32[]{:S(2)}) copy-start(f32[1024,128]{1,0:T(8,128)} %get-tuple-element.40.link_ref) | copy-start | bytes 1572868
  40.9 0.7 %copy-start.8 = (f32[16,128]{1,0:T(8,128)S(1)}, f32[16,128]{1,0:T(8,128)}, u32[]{:S(2)}) copy-start(f32[16,128]{1,0:T(8,128)} %get-tuple-element.39.peak_ref) | copy-start | bytes 24580

commit v3 on v2

--- a/solution.py
+++ b/solution.py
@@ -14,7 +14,7 @@
 D = 0.2
 CENTRE = 1.0 - 4.0 * D
 F32 = jnp.float32
-SOLVE_LIMIT = 54 * 1024 * 1024
+SOLVE_LIMIT = 53 * 1024 * 1024 + 512 * 1024
 VMEM_LIMIT = 8 * 1024 * 1024
 
 
@@ -113,9 +113,9 @@
 
 
 def solve_kernel(
-    partner_ref, flip_ref, adj_hbm, kap_hbm, depth_hbm, vel_hbm, tan_hbm, forcing_hbm,
-    edge_ref, depth_ref, table_ref, solved_hbm, peak_ref, link_ref,
-    coup, given, part, solved, adj_ref, kap_ref, forcing_ref, vel_ref, tan_ref, done,
+    partner_ref, flip_ref, adj_hbm, kap_hbm, depth_hbm, vel_hbm, tan_hbm, forcing_hbm, base_hbm,
+    edge_ref, depth_ref, table_ref, solved_hbm, peak_ref, link_hbm,
+    coup, given, part, solved, link_ref, adj_ref, kap_ref, forcing_ref, vel_ref, tan_ref, base_ref, done,
 ):
     copies = [
         pltpu.make_async_copy(source, target, done.at[number])
@@ -127,6 +127,7 @@
                 (forcing_hbm, forcing_ref),
                 (vel_hbm, vel_ref),
                 (tan_hbm, tan_ref),
+                (base_hbm, base_ref),
             )
         )
     ]
@@ -174,6 +175,8 @@
 
     zero = jnp.zeros((8, 128), F32)
     lax.fori_loop(0, GROUPS, forward, (zero + 1.0, zero, zero, zero))
+    keep_link = pltpu.make_async_copy(link_ref, link_hbm, done.at[8])
+    keep_link.start()
 
     def backward(n, carry):
         x_t, x_s = carry
@@ -191,12 +194,20 @@
     x_t, x_s = lax.fori_loop(0, GROUPS, backward, (zero, zero))
     peak_ref[0:8, :] = x_t
     peak_ref[8:16, :] = x_s
-    keep = pltpu.make_async_copy(solved, solved_hbm, done.at[6])
+    keep = pltpu.make_async_copy(solved, solved_hbm, done.at[7])
     keep.start()
     copies[3].wait()
     make_table(forcing_ref, table_ref)
     for copy in copies[4:]:
         copy.wait()
+    for t in range(2):
+        for c, piece in enumerate(pieces_of(base_ref, slice(t, t + 1))):
+            peak_ref[16 + 8 * t + c : 17 + 8 * t + c, :] = piece
+        for c, piece in enumerate(pieces_of(tan_ref, t, slice(0, 1))):
+            wet = depths[c] > 0
+            peak_ref[32 + 8 * t + c : 33 + 8 * t + c, :] = jnp.where(wet, piece, 0.0)
+    for c, piece in enumerate(depths):
+        peak_ref[48 + c : 49 + c, :] = piece.astype(F32)
 
     small = lanes(8, 128)
     south, north = flip_ref[0, 2] == 1, flip_ref[0, 3] == 1
@@ -246,10 +257,11 @@
     )
     edge_ref[128:136, :] = jnp.where(small < 120, target, -1).astype(F32)
     keep.wait()
+    keep_link.wait()
 
 
 def stencil_kernel(
-    flip_ref, tan_ref, vel_ref, depth_ref, base_ref, solved, rhs_ref, back_ref, rim_ref,
+    flip_ref, tan_ref, vel_ref, depth_ref, solved, rhs_ref, back_ref, rim_ref,
 ):
     depth = wide(depth_ref, slice(0, 1))
     sub = lax.broadcasted_iota(jnp.int32, (8, WIDE), 0)
@@ -309,26 +321,22 @@
         return carry
 
     lax.fori_loop(0, GROUPS, stencil, 0)
-    wet = 0 < depth
-    for t in range(2):
-        first = wide(tan_ref, t, slice(0, 1))
-        for c, piece in enumerate(split(jnp.where(wet, first, 0.0))):
-            rim_ref[192 + 8 * t + c : 193 + 8 * t + c, :] = piece
-        for c, piece in enumerate(pieces_of(base_ref, slice(t, t + 1))):
-            rim_ref[208 + 8 * t + c : 209 + 8 * t + c, :] = piece
-    for c, piece in enumerate(split(depth)):
-        rim_ref[224 + c : 225 + c, :] = piece.astype(F32)
-
-
-def route_kernel(e0, e1, e2, e3, out_ref):
+
+
+def route_kernel(e0, e1, e2, e3, out_hbm, slots, done):
     mine = lax.shift_right_logical(lax.axis_index("tile"), 3)
     sources = (e0, e1, e2, e3)
     goals = [ref[128:129, :].astype(jnp.int32) for ref in sources]
+    copies = []
     for b in range(8):
         total = jnp.zeros((128, 128), F32)
         for goal, ref in zip(goals, sources):
             total = jnp.where(goal == 8 * mine + b, ref[0:128, :], total)
-        out_ref[b] = total
+        slots[b] = total
+        copies.append(pltpu.make_async_copy(slots.at[b], out_hbm.at[b], done.at[b]))
+        copies[-1].start()
+    for copy in copies:
+        copy.wait()
 
 
 def finish_kernel(
@@ -342,12 +350,12 @@
     carrier, scaled, loss = [
         sum(ref[8 * f : 8 * f + 8, :] for ref in (r0, r1, r2, r3)) for f in range(3)
     ]
-    moist = scaled * jnp.exp(0.5 * rim_ref[208:216, :])
-    wet = rim_ref[224:232, :] > 0.0
+    moist = scaled * jnp.exp(0.5 * peak_ref[16:24, :])
+    wet = peak_ref[48:56, :] > 0.0
     heat_self = jnp.where(wet, -(0.5 * carrier + 0.25 * moist), 0.0)
-    salt_heat = jnp.where(wet, 0.25 * rim_ref[216:224, :] * moist, 0.0)
+    salt_heat = jnp.where(wet, 0.25 * peak_ref[24:32, :] * moist, 0.0)
     salt_self = jnp.where(wet, 0.5 * moist - loss, 0.0)
-    tan_t, tan_s = rim_ref[192:200, :], rim_ref[200:208, :]
+    tan_t, tan_s = peak_ref[32:40, :], peak_ref[40:48, :]
     adj_t, adj_s = peak_ref[0:8, :], peak_ref[8:16, :]
 
     small = lanes(8, 128)
@@ -414,34 +422,29 @@
 
     lax.fori_loop(0, GROUPS, forward, (zero, zero, zero))
 
-    def backward(n, carry):
-        x_t, x_s = carry
-        i = GROUPS - 1 - n
+    x_t = x_s = zero
+    copies = [copy_prev]
+    for i in reversed(range(GROUPS)):
         for s in reversed(range(8)):
             strided = pl.ds(64 * i + s, 8, stride=8)
-            packed = pl.ds(pl.multiple_of(64 * i + 8 * s, 8), 8)
+            packed = pl.ds(64 * i + 8 * s, 8)
             m = link_ref[packed, :]
             x_t = part[0, packed, :] + m * x_t
             x_s = part[1, packed, :] + m * x_s
             solved[0, strided, :] = x_t
             solved[1, strided, :] = x_s
-        return x_t, x_s
-
-    lax.fori_loop(0, GROUPS, backward, (zero, zero))
-
-    def write(i, carry):
-        rows = pl.ds(pl.multiple_of(8 * i, 8), 8)
-        at = pl.multiple_of(64 * i, 64)
+        rows = pl.ds(8 * i, 8)
         for t in range(2):
             for c in range(CHUNKS):
-                put_piece(next_ref, t, rows, c, solved[t, pl.ds(at + 8 * c, 8), :])
-        return carry
-
-    lax.fori_loop(0, GROUPS, write, 0)
-    copy_next = pltpu.make_async_copy(next_ref, next_hbm, done.at[1])
-    copy_next.start()
-    copy_next.wait()
-    copy_prev.wait()
+                put_piece(next_ref, t, rows, c, solved[t, pl.ds(64 * i + 8 * c, 8), :])
+        copies.append(
+            pltpu.make_async_copy(
+                next_ref.at[:, rows, :], next_hbm.at[:, rows, :], done.at[3 + i]
+            )
+        )
+        copies[-1].start()
+    for copy in copies:
+        copy.wait()
 
 
 def call(kernel, name, micros, ins, outs, scratch=(), limit=VMEM_LIMIT):
@@ -503,23 +506,25 @@
         solve_kernel,
         "solve",
         4.0,
-        "SSHHHHHH",
+        "SSHHHHHHH",
         [("V", (136, 128)), ("V", line), ("V", (384, 128))]
-        + [("H", blocked), ("V", (16, 128)), ("V", (16 * Z, 128))],
+        + [("H", blocked), ("V", (56, 128)), ("H", (16 * Z, 128))],
         [
             pltpu.VMEM(flat, F32),
             pltpu.VMEM(blocked, F32),
             pltpu.VMEM(blocked, F32),
             pltpu.VMEM(blocked, F32),
+            pltpu.VMEM((16 * Z, 128), F32),
             pltpu.VMEM(natural, F32),
             pltpu.VMEM((Z - 1, 1, CELLS), F32),
             pltpu.VMEM((1024, 128), F32),
             pltpu.VMEM(natural, F32),
             pltpu.VMEM(natural, F32),
-            pltpu.SemaphoreType.DMA((7,)),
+            pltpu.VMEM((2, CELLS), F32),
+            pltpu.SemaphoreType.DMA((9,)),
         ],
         limit=SOLVE_LIMIT,
-    )(partner, flip, adjoint, kappa, depth, velocity, tangent, banded)
+    )(partner, flip, adjoint, kappa, depth, velocity, tangent, banded, base)
     table, edges, asked = lax.optimization_barrier((table, edges, asked))
     mate = swap(table, "region", 8, 1)
     edge = [edges] + [swap(edges, "tile", 32, k) for k in (8, 16, 24)]
@@ -539,7 +544,14 @@
     ]
 
     edge[0], first = lax.optimization_barrier((edge[0], answers[0]))
-    (slots,) = call(route_kernel, "route", 0.9, "VVVV", [("V", (8, 128, 128))])(*edge)
+    (slots,) = call(
+        route_kernel,
+        "route",
+        0.9,
+        "VVVV",
+        [("H", (8, 128, 128))],
+        [pltpu.VMEM((8, 128, 128), F32), pltpu.SemaphoreType.DMA((8,))],
+    )(*edge)
     groups = [[8 * a + b for b in range(8)] for a in range(4)]
     arrived = lax.all_to_all(slots, "tile", 0, 0, axis_index_groups=groups, tiled=True)
 
@@ -547,9 +559,9 @@
         stencil_kernel,
         "stencil",
         3.0,
-        "SVVVVV",
-        [("V", blocked), ("V", natural), ("V", (232, 128))],
-    )(flip, tangent, velocity, depth, base, solved)
+        "SVVVV",
+        [("V", blocked), ("V", natural), ("V", (192, 128))],
+    )(flip, tangent, velocity, depth, solved)
 
     following, previous = call(
         finish_kernel,
@@ -563,7 +575,7 @@
             pltpu.VMEM(blocked, F32),
             pltpu.VMEM(natural, F32),
             pltpu.VMEM(natural, F32),
-            pltpu.SemaphoreType.DMA((3,)),
+            pltpu.SemaphoreType.DMA((11,)),
         ],
     )(arrived, rhs, back, rim, peak, link, *replies, depth)
     return following[None, None], previous[None, None]

time: 44 us -> 43.2 us (0.982)
  waiting for transfers between devices: 3.05 us -> 4.94 us
  Pallas kernels: 13.6 us -> 12.2 us
  local copies, waits for them, and re-layouts: 2.63 us -> 1.76 us
    pallas_call x3, Pallas kernels: 8.83 us -> 7.68 us  [the longest x1 3.48 us: shards(): call(solve_kernel, 'solve', 4.0, 'SSHHHHHHH', [('V', (136, 128)), ('V', l...]
    unnamed x22 -> x18, local copies, waits for them, and re-layouts: 2.63 us -> 1.76 us
    ppermute x3, waiting for transfers between devices: 0.66 us -> 1.42 us  [shards(): lax.ppermute(value, both, [(target, source) for source, target in way])]
    ppermute x4, waiting for transfers between devices: 1.98 us -> 2.7 us  [swap(): return lax.ppermute(value, axis, [(i, i ^ bit) for i in range(size)])]
    ppermute x3, starting transfers between devices: 6.33 us -> 5.85 us  [shards(): lax.ppermute(value, both, [(target, source) for source, target in way])]
  transfers between devices with their start and end apart: 11 -> 11, of which waited for: 3 -> 4; matrix products, arithmetic and copies ran while one was open for 0% -> 0% of each run, Pallas kernels for 24% -> 22%
where the time goes in v3:
time: 43.2 us; the launch traced here: 42.9 us
  starting transfers between devices  23.2 us (54%)
  Pallas kernels  12.2 us (28%)
  waiting for transfers between devices  4.94 us (11%)
  local copies, waits for them, and re-layouts  1.76 us (4%)
  between operations  0.74 us (2%)
    ppermute x3, starting transfers between devices, shards(): asked = [lax.ppermute(mine, both, way) for way in hops()]  8.31 us
    ppermute x3, starting transfers between devices, shards(): lax.ppermute(value, both, [(target, source) for source, target in way])  5.85 us
    all_to_all x1, starting transfers between devices, shards(): lax.all_to_all(slots, 'tile', 0, 0, axis_index_groups=groups, tiled=True)  4.92 us
    ppermute x4, starting transfers between devices, swap(): return lax.ppermute(value, axis, [(i, i ^ bit) for i in range(size)])  4.1 us
    pallas_call x1, Pallas kernels, shards(): call(solve_kernel, 'solve', 4.0, 'SSHHHHHHH', [('V', (136, 128)), ('V', l...  3.48 us
    pallas_call x1, Pallas kernels, shards(): call(stencil_kernel, 'stencil', 3.0, 'SVVVV', [('V', blocked), ('V', natu...  3.3 us
    pallas_call x1, Pallas kernels, shards(): call(lookup_kernel, 'lookup', 2.7, 'V' * 6, [('V', answer)] * 4, [pltpu.V...  2.73 us
    ppermute x4, waiting for transfers between devices, swap(): return lax.ppermute(value, axis, [(i, i ^ bit) for i in range(size)])  2.7 us
  transfers between devices with their start and end apart: 11, of which 4 were waited for; matrix products, arithmetic and copies ran while one was open for 0% of the time, Pallas kernels for 22%

profile of v3, /device:TPU:6, one launch (start us, length us, event | category | flops | bytes accessed | tf_op | source)
XLA Modules:
  0.0 42.9 jit_solution(5562916514816338386)
XLA Ops:
  0.6 6.8 %collective-permute-start.2 = (s32[1,900]{1,0:T(1,128)}, s32[1,900]{1,0:T(1,128)S(1)}, u32[]{:S(2)}, u32[]{:S(2)}) collective-permute-start(s32[1,900]{1,0:T(1,128)} %bitcast.22), channel_id=1, source_target_pairs={{0,129},{2,131},{4,133},{6,135},{8,137},{10,139},{12,141},{14,143}... | collective-permute-start | bytes 10808 | tf_op jit(solution)/shard_map/ppermute | solution.py:503
  7.5 1.5 %collective-permute-start.1 = (s32[1,900]{1,0:T(1,128)}, s32[1,900]{1,0:T(1,128)S(1)}, u32[]{:S(2)}, u32[]{:S(2)}) collective-permute-start(s32[1,900]{1,0:T(1,128)} %bitcast.23), channel_id=1, source_target_pairs={{0,64},{2,66},{4,68},{6,70},{8,72},{10,74},{12,76},{14,78},{16,80}... | collective-permute-start | bytes 10808 | tf_op jit(solution)/shard_map/ppermute | solution.py:503
  8.9 0.0 collective-permute-start
  9.0 0.7 %copy-done.4 = f32[1,1,2,900]{3,2,1,0:T(2,128)S(1)} copy-done((f32[1,1,2,900]{3,2,1,0:T(2,128)S(1)}, f32[1,1,2,900]{3,2,1,0:T(2,128)}, u32[]{:S(2)}) %copy-start.4) | copy-done | bytes 7224
  9.6 0.0 copy-done.5
  9.7 3.5 %solve.1 = (f32[136,128]{1,0:T(8,128)S(1)}, s32[1,900]{1,0:T(1,128)S(1)}, f32[384,128]{1,0:T(8,128)S(1)}, f32[2,512,128]{2,1,0:T(8,128)}, f32[56,128]{1,0:T(8,128)S(1)}, /*index=5*/f32[1024,128]{1,0:T(8,128)}) custom-call(s32[1,4]{1,0:T(1,128)S(1)} %bitcast.28, s32[1,4]{1,0:T(1,128)S(1)} %bitcast.26, f32[2,64,900]{2,1,0:T(8,128)} %bitcast.29, ...), custom_call_target="tpu_custom_call" | custom-call | bytes 14760000 | tf_op jit(solution)/shard_map/solve/pallas_call | solution.py:505
  13.1 0.2 collective-permute-done.1.q2
  13.4 0.6 %collective-permute-done.q1 = s32[1,900]{1,0:T(1,128)S(1)} collective-permute-done((s32[1,900]{1,0:T(1,128)}, s32[1,900]{1,0:T(1,128)S(1)}, u32[]{:S(2)}, u32[]{:S(2)}) %collective-permute-start) | collective-permute-done | bytes 3632 | tf_op jit(solution)/shard_map/ppermute | solution.py:503
  14.0 3.0 %collective-permute-start.6 = (f32[136,128]{1,0:T(8,128)S(1)}, f32[136,128]{1,0:T(8,128)S(1)}, u32[]{:S(2)}, u32[]{:S(2)}) collective-permute-start(f32[136,128]{1,0:T(8,128)S(1)} %get-tuple-element.33.e0), channel_id=1, source_target_pairs={{0,24},{1,25},{2,26},{3,27},{4,28},{5,29},{6,30},{7,31},{8,16},{9,... | collective-permute-start | bytes 208904 | tf_op jit(solution)/shard_map/ppermute | solution.py:471
  17.0 0.6 %collective-permute-start.5 = (f32[136,128]{1,0:T(8,128)S(1)}, f32[136,128]{1,0:T(8,128)S(1)}, u32[]{:S(2)}, u32[]{:S(2)}) collective-permute-start(f32[136,128]{1,0:T(8,128)S(1)} %get-tuple-element.33.e0), channel_id=1, source_target_pairs={{0,16},{1,17},{2,18},{3,19},{4,20},{5,21},{6,22},{7,23},{8,24},{9,... | collective-permute-start | bytes 208904 | tf_op jit(solution)/shard_map/ppermute | solution.py:471
  17.6 0.5 %collective-permute-start.4 = (f32[136,128]{1,0:T(8,128)S(1)}, f32[136,128]{1,0:T(8,128)S(1)}, u32[]{:S(2)}, u32[]{:S(2)}) collective-permute-start(f32[136,128]{1,0:T(8,128)S(1)} %get-tuple-element.33.e0), channel_id=1, source_target_pairs={{0,8},{1,9},{2,10},{3,11},{4,12},{5,13},{6,14},{7,15},{8,0},{9,1},... | collective-permute-start | bytes 208904 | tf_op jit(solution)/shard_map/ppermute | solution.py:471
  18.1 2.7 %lookup.1 = (f32[24,128]{1,0:T(8,128)S(1)}, f32[24,128]{1,0:T(8,128)S(1)}, f32[24,128]{1,0:T(8,128)S(1)}, f32[24,128]{1,0:T(8,128)S(1)}) custom-call(f32[384,128]{1,0:T(8,128)S(1)} %get-tuple-element.28.own_ref, f32[384,128]{1,0:T(8,128)S(1)} %collective-permute-done.3.mate_ref, s32[1,900]{1,0:T(1,128)S(1)} %bitcast.25, ...), custom_call_target="tpu_custom_call" | custom-call | bytes 9963000 | tf_op jit(solution)/shard_map/lookup/pallas_call | solution.py:533
  20.8 2.7 %collective-permute-done.5.e2 = f32[136,128]{1,0:T(8,128)S(1)} collective-permute-done((f32[136,128]{1,0:T(8,128)S(1)}, f32[136,128]{1,0:T(8,128)S(1)}, u32[]{:S(2)}, u32[]{:S(2)}) %collective-permute-start.5) | collective-permute-done | bytes 69664 | tf_op jit(solution)/shard_map/ppermute | solution.py:471
  23.5 0.9 %route.1 = f32[8,128,128]{2,1,0:T(8,128)} custom-call(f32[136,128]{1,0:T(8,128)S(1)} %get-tuple-element.33.e0, f32[136,128]{1,0:T(8,128)S(1)} %collective-permute-done.4.e1, f32[136,128]{1,0:T(8,128)S(1)} %collective-permute-done.5.e2, f32[136,128]{1,0:T(8,128)S(1)} %collective-permute-done.6.e3), custom_call_target="tpu_custom_call" | custom-call | bytes 3321000 | tf_op jit(solution)/shard_map/route/pallas_call | solution.py:547
  24.4 0.0 copy-start
  24.4 0.0 copy-start.1
  24.4 4.9 %all-to-all-start = ((f32[8,128,128]{2,1,0:T(8,128)}), f32[8,128,128]{2,1,0:T(8,128)S(1)}, u32[]{:S(2)}, u32[]{:S(2)}) async-start(f32[8,128,128]{2,1,0:T(8,128)} %route.1), calls=%async_computation | async-start | bytes 1048576 | tf_op jit(solution)/shard_map/all_to_all | solution.py:556
  29.4 3.5 %collective-permute-start.7 = (f32[24,128]{1,0:T(8,128)S(1)}, f32[24,128]{1,0:T(8,128)S(1)}, u32[]{:S(2)}, u32[]{:S(2)}) collective-permute-start(f32[24,128]{1,0:T(8,128)S(1)} %get-tuple-element.41), channel_id=1, source_target_pairs={{193,0},{195,2},{197,4},{199,6},{201,8},{203,10},{205,12},{207,14}... | collective-permute-start | bytes 36872 | tf_op jit(solution)/shard_map/ppermute | solution.py:542
  32.8 1.5 %collective-permute-start.8 = (f32[24,128]{1,0:T(8,128)S(1)}, f32[24,128]{1,0:T(8,128)S(1)}, u32[]{:S(2)}, u32[]{:S(2)}) collective-permute-start(f32[24,128]{1,0:T(8,128)S(1)} %get-tuple-element.42), channel_id=1, source_target_pairs={{64,0},{66,2},{68,4},{70,6},{72,8},{74,10},{76,12},{78,14},{80,16}... | collective-permute-start | bytes 36872 | tf_op jit(solution)/shard_map/ppermute | solution.py:542
  34.3 0.9 %collective-permute-start.9 = (f32[24,128]{1,0:T(8,128)S(1)}, f32[24,128]{1,0:T(8,128)S(1)}, u32[]{:S(2)}, u32[]{:S(2)}) collective-permute-start(f32[24,128]{1,0:T(8,128)S(1)} %get-tuple-element.43), channel_id=1, source_target_pairs={{129,0},{131,2},{133,4},{135,6},{137,8},{139,10},{141,12},{143,14}... | collective-permute-start | bytes 36872 | tf_op jit(solution)/shard_map/ppermute | solution.py:542
  35.2 1.0 %copy-done.3 = f32[2,512,128]{2,1,0:T(8,128)S(1)} copy-done((f32[2,512,128]{2,1,0:T(8,128)S(1)}, f32[2,512,128]{2,1,0:T(8,128)}, u32[]{:S(2)}) %copy-start.3) | copy-done | bytes 524312
  36.3 3.3 %stencil.1 = (f32[2,512,128]{2,1,0:T(8,128)S(1)}, f32[2,64,900]{2,1,0:T(8,128)S(1)}, f32[192,128]{1,0:T(8,128)S(1)}) custom-call(s32[1,4]{1,0:T(1,128)S(1)} %bitcast.27, f32[2,64,900]{2,1,0:T(8,128)S(1)} %bitcast.19, f32[2,64,900]{2,1,0:T(8,128)S(1)} %bitcast.17, s32[1,900]{1,0:T(1,128)S(1)} %get-tuple-element.34.depth_ref, f32[2,512,128]{2,1,0:T(8,128)S(1)} %copy-done.3), custom_call_target="tpu_custom_call" | custom-call | bytes 11070000 | tf_op jit(solution)/shard_map/stencil/pallas_call | solution.py:558
  39.6 1.4 %collective-permute-done.9.r3 = f32[24,128]{1,0:T(8,128)S(1)} collective-permute-done((f32[24,128]{1,0:T(8,128)S(1)}, f32[24,128]{1,0:T(8,128)S(1)}, u32[]{:S(2)}, u32[]{:S(2)}) %collective-permute-start.9) | collective-permute-done | bytes 12320 | tf_op jit(solution)/shard_map/ppermute | solution.py:542
  41.0 1.8 %finish.1 = (f32[2,64,900]{2,1,0:T(8,128)}, f32[2,64,900]{2,1,0:T(8,128)}) custom-call(f32[8,128,128]{2,1,0:T(8,128)S(1)} %all-to-all-done.edge_ref, f32[2,512,128]{2,1,0:T(8,128)S(1)} %get-tuple-element.36.rhs_ref, f32[2,64,900]{2,1,0:T(8,128)S(1)} %get-tuple-element.37.back_hbm, f32[192,128]{1,0:T(8,128)S(1)} %get-tuple-element.38.rim_ref, ...), custom_call_target="tpu_custom_call" | custom-call | bytes 7749000 | tf_op jit(solution)/shard_map/finish/pallas_call | solution.py:566
  (21 shorter events, 0.0 us)
Async XLA Ops:
  0.6 12.5 %collective-permute-start.2 = (s32[1,900]{1,0:T(1,128)}, s32[1,900]{1,0:T(1,128)S(1)}, u32[]{:S(2)}, u32[]{:S(2)}) collective-permute-start(s32[1,900]{1,0:T(1,128)} %bitcast.22), channel_id=1, source_target_pairs={{0,129},{2,131},{4,133},{6,135},{8,137},{10,139},{12,141},{14,143}... | collective-permute-start | bytes 10808 | tf_op jit(solution)/shard_map/ppermute | solution.py:503
  7.5 5.9 %collective-permute-start.1 = (s32[1,900]{1,0:T(1,128)}, s32[1,900]{1,0:T(1,128)S(1)}, u32[]{:S(2)}, u32[]{:S(2)}) collective-permute-start(s32[1,900]{1,0:T(1,128)} %bitcast.23), channel_id=1, source_target_pairs={{0,64},{2,66},{4,68},{6,70},{8,72},{10,74},{12,76},{14,78},{16,80}... | collective-permute-start | bytes 10808 | tf_op jit(solution)/shard_map/ppermute | solution.py:503
  8.9 5.0 %collective-permute-start = (s32[1,900]{1,0:T(1,128)}, s32[1,900]{1,0:T(1,128)S(1)}, u32[]{:S(2)}, u32[]{:S(2)}) collective-permute-start(s32[1,900]{1,0:T(1,128)} %bitcast.24), channel_id=1, source_target_pairs={{0,193},{2,195},{4,197},{6,199},{8,201},{10,203},{12,205},{14,207}... | collective-permute-start | bytes 10808 | tf_op jit(solution)/shard_map/ppermute | solution.py:503
  8.9 0.7 %copy-start.4 = (f32[1,1,2,900]{3,2,1,0:T(2,128)S(1)}, f32[1,1,2,900]{3,2,1,0:T(2,128)}, u32[]{:S(2)}) copy-start(f32[1,1,2,900]{3,2,1,0:T(2,128)} %param.12) | copy-start | bytes 21604
  8.9 0.7 %copy-start.5 = (s32[1,1,900]{2,1,0:T(1,128)S(1)}, s32[1,1,900]{2,1,0:T(1,128)}, u32[]{:S(2)}) copy-start(s32[1,1,900]{2,1,0:T(1,128)} %param.15) | copy-start | bytes 10804
  8.9 0.7 %copy-start.7 = (s32[1,1,4]{2,1,0:T(1,128)S(1)}, s32[1,1,4]{2,1,0:T(1,128)}, u32[]{:S(2)}) copy-start(s32[1,1,4]{2,1,0:T(1,128)} %param.19) | copy-start | bytes 52
  9.0 0.7 %copy-start.8 = (s32[1,1,4]{2,1,0:T(1,128)S(1)}, s32[1,1,4]{2,1,0:T(1,128)}, u32[]{:S(2)}) copy-start(s32[1,1,4]{2,1,0:T(1,128)} %param.18) | copy-start | bytes 52
  9.7 8.4 %copy-start.6 = (s32[1,1,900]{2,1,0:T(1,128)S(1)}, s32[1,1,900]{2,1,0:T(1,128)}, u32[]{:S(2)}) copy-start(s32[1,1,900]{2,1,0:T(1,128)} %param.17) | copy-start | bytes 10804
  14.0 4.1 %collective-permute-start.3 = (f32[384,128]{1,0:T(8,128)S(1)}, f32[384,128]{1,0:T(8,128)S(1)}, u32[]{:S(2)}, u32[]{:S(2)}) collective-permute-start(f32[384,128]{1,0:T(8,128)S(1)} %get-tuple-element.28.own_ref), channel_id=1, source_target_pairs={{0,32},{32,0},{64,96},{96,64},{128,160},{160,128},{192,224},{224,1... | collective-permute-start | bytes 589832 | tf_op jit(solution)/shard_map/ppermute | solution.py:471
  14.0 6.8 %collective-permute-start.6 = (f32[136,128]{1,0:T(8,128)S(1)}, f32[136,128]{1,0:T(8,128)S(1)}, u32[]{:S(2)}, u32[]{:S(2)}) collective-permute-start(f32[136,128]{1,0:T(8,128)S(1)} %get-tuple-element.33.e0), channel_id=1, source_target_pairs={{0,24},{1,25},{2,26},{3,27},{4,28},{5,29},{6,30},{7,31},{8,16},{9,... | collective-permute-start | bytes 208904 | tf_op jit(solution)/shard_map/ppermute | solution.py:471
  17.0 6.5 %collective-permute-start.5 = (f32[136,128]{1,0:T(8,128)S(1)}, f32[136,128]{1,0:T(8,128)S(1)}, u32[]{:S(2)}, u32[]{:S(2)}) collective-permute-start(f32[136,128]{1,0:T(8,128)S(1)} %get-tuple-element.33.e0), channel_id=1, source_target_pairs={{0,16},{1,17},{2,18},{3,19},{4,20},{5,21},{6,22},{7,23},{8,24},{9,... | collective-permute-start | bytes 208904 | tf_op jit(solution)/shard_map/ppermute | solution.py:471
  17.6 5.9 %collective-permute-start.4 = (f32[136,128]{1,0:T(8,128)S(1)}, f32[136,128]{1,0:T(8,128)S(1)}, u32[]{:S(2)}, u32[]{:S(2)}) collective-permute-start(f32[136,128]{1,0:T(8,128)S(1)} %get-tuple-element.33.e0), channel_id=1, source_target_pairs={{0,8},{1,9},{2,10},{3,11},{4,12},{5,13},{6,14},{7,15},{8,0},{9,1},... | collective-permute-start | bytes 208904 | tf_op jit(solution)/shard_map/ppermute | solution.py:471
  24.4 10.8 %copy-start = (f32[1,1,2,64,900]{4,3,2,1,0:T(8,128)S(1)}, f32[1,1,2,64,900]{4,3,2,1,0:T(8,128)}, u32[]{:S(2)}) copy-start(f32[1,1,2,64,900]{4,3,2,1,0:T(8,128)} %param.13) | copy-start | bytes 1382404
  24.4 10.8 %copy-start.1 = (f32[1,1,2,64,900]{4,3,2,1,0:T(8,128)S(1)}, f32[1,1,2,64,900]{4,3,2,1,0:T(8,128)}, u32[]{:S(2)}) copy-start(f32[1,1,2,64,900]{4,3,2,1,0:T(8,128)} %param.10) | copy-start | bytes 1382404
  24.4 16.6 %all-to-all-start = ((f32[8,128,128]{2,1,0:T(8,128)}), f32[8,128,128]{2,1,0:T(8,128)S(1)}, u32[]{:S(2)}, u32[]{:S(2)}) async-start(f32[8,128,128]{2,1,0:T(8,128)} %route.1), calls=%async_computation | async-start | bytes 1048576 | tf_op jit(solution)/shard_map/all_to_all | solution.py:556
  29.4 10.2 %collective-permute-start.7 = (f32[24,128]{1,0:T(8,128)S(1)}, f32[24,128]{1,0:T(8,128)S(1)}, u32[]{:S(2)}, u32[]{:S(2)}) collective-permute-start(f32[24,128]{1,0:T(8,128)S(1)} %get-tuple-element.41), channel_id=1, source_target_pairs={{193,0},{195,2},{197,4},{199,6},{201,8},{203,10},{205,12},{207,14}... | collective-permute-start | bytes 36872 | tf_op jit(solution)/shard_map/ppermute | solution.py:542
  32.8 6.7 %collective-permute-start.8 = (f32[24,128]{1,0:T(8,128)S(1)}, f32[24,128]{1,0:T(8,128)S(1)}, u32[]{:S(2)}, u32[]{:S(2)}) collective-permute-start(f32[24,128]{1,0:T(8,128)S(1)} %get-tuple-element.42), channel_id=1, source_target_pairs={{64,0},{66,2},{68,4},{70,6},{72,8},{74,10},{76,12},{78,14},{80,16}... | collective-permute-start | bytes 36872 | tf_op jit(solution)/shard_map/ppermute | solution.py:542
  34.3 6.7 %collective-permute-start.9 = (f32[24,128]{1,0:T(8,128)S(1)}, f32[24,128]{1,0:T(8,128)S(1)}, u32[]{:S(2)}, u32[]{:S(2)}) collective-permute-start(f32[24,128]{1,0:T(8,128)S(1)} %get-tuple-element.43), channel_id=1, source_target_pairs={{129,0},{131,2},{133,4},{135,6},{137,8},{139,10},{141,12},{143,14}... | collective-permute-start | bytes 36872 | tf_op jit(solution)/shard_map/ppermute | solution.py:542
  35.2 1.0 %copy-start.3 = (f32[2,512,128]{2,1,0:T(8,128)S(1)}, f32[2,512,128]{2,1,0:T(8,128)}, u32[]{:S(2)}) copy-start(f32[2,512,128]{2,1,0:T(8,128)} %get-tuple-element.35.solved) | copy-start | bytes 1572868
  36.3 4.7 %copy-start.2 = (f32[1024,128]{1,0:T(8,128)S(1)}, f32[1024,128]{1,0:T(8,128)}, u32[]{:S(2)}) copy-start(f32[1024,128]{1,0:T(8,128)} %get-tuple-element.40.link_ref) | copy-start | bytes 1572868

commit v4 on v3

--- a/solution.py
+++ b/solution.py
@@ -15,6 +15,7 @@
 CENTRE = 1.0 - 4.0 * D
 F32 = jnp.float32
 SOLVE_LIMIT = 53 * 1024 * 1024 + 512 * 1024
+STENCIL_LIMIT = 51 * 1024 * 1024 + 640 * 1024
 VMEM_LIMIT = 8 * 1024 * 1024
 
 
@@ -261,8 +262,11 @@
 
 
 def stencil_kernel(
-    flip_ref, tan_ref, vel_ref, depth_ref, solved, rhs_ref, back_ref, rim_ref,
+    flip_ref, tan_ref, vel_ref, depth_ref, solved_hbm, rhs_ref, back_ref, rim_ref,
+    solved, done,
 ):
+    fetch = pltpu.make_async_copy(solved_hbm, solved, done.at[0])
+    fetch.start()
     depth = wide(depth_ref, slice(0, 1))
     sub = lax.broadcasted_iota(jnp.int32, (8, WIDE), 0)
     x0, x29, y0, y29 = grid_masks(8)
@@ -292,7 +296,26 @@
             mixed = jnp.where(wet, mixed, 0.0)
             for c, piece in enumerate(split(mixed)):
                 rhs_ref[t, pl.ds(at + 8 * c, 8), :] = piece
-
+        wet, to_n, to_s = split(wet), split(to_n), split(to_s)
+        rim = (
+            jnp.where(jnp.logical_and(wet[0], small < SIDE), to_s[0], 0.0),
+            jnp.where(jnp.logical_and(wet[6], small >= 102), to_n[6], 0.0),
+            jnp.where(jnp.logical_and(wet[7], small < 4), to_n[7], 0.0),
+        )
+        for number, piece in enumerate(rim):
+            rim_ref[pl.ds(pl.multiple_of(64 * number + 8 * i, 8), 8), :] = piece
+        return carry
+
+    lax.fori_loop(0, GROUPS, stencil, 0)
+    fetch.wait()
+
+    def adjoint(i, carry):
+        rows = pl.ds(pl.multiple_of(8 * i, 8), 8)
+        at = pl.multiple_of(64 * i, 64)
+        wet = sub + 8 * i < depth
+        half_x, half_y = 0.5 * wide(vel_ref, 0, rows), 0.5 * wide(vel_ref, 1, rows)
+        to_e, to_w, to_n, to_s = D - half_x, D + half_x, D - half_y, D + half_y
+        for t in range(2):
             answer = jnp.concatenate(
                 [solved[t, pl.ds(at + 8 * c, 8), :] for c in range(CHUNKS)], axis=1
             )
@@ -310,17 +333,9 @@
             inner = jnp.where(wet, inner, 0.0)
             for c, piece in enumerate(split(inner)):
                 put_piece(back_ref, t, rows, c, piece)
-        wet, to_n, to_s = split(wet), split(to_n), split(to_s)
-        rim = (
-            jnp.where(jnp.logical_and(wet[0], small < SIDE), to_s[0], 0.0),
-            jnp.where(jnp.logical_and(wet[6], small >= 102), to_n[6], 0.0),
-            jnp.where(jnp.logical_and(wet[7], small < 4), to_n[7], 0.0),
-        )
-        for number, piece in enumerate(rim):
-            rim_ref[pl.ds(pl.multiple_of(64 * number + 8 * i, 8), 8), :] = piece
         return carry
 
-    lax.fori_loop(0, GROUPS, stencil, 0)
+    lax.fori_loop(0, GROUPS, adjoint, 0)
 
 
 def route_kernel(e0, e1, e2, e3, out_hbm, slots, done):
@@ -540,7 +555,7 @@
     )(table, mate, mine, *asked)
     replies = [answers[0]] + [
         lax.ppermute(value, both, [(target, source) for source, target in way])
-        for value, way in zip(answers[1:], hops())
+        for value, way in reversed(list(zip(answers[1:], hops())))
     ]
 
     edge[0], first = lax.optimization_barrier((edge[0], answers[0]))
@@ -559,8 +574,10 @@
         stencil_kernel,
         "stencil",
         3.0,
-        "SVVVV",
+        "SVVVH",
         [("V", blocked), ("V", natural), ("V", (192, 128))],
+        [pltpu.VMEM(blocked, F32), pltpu.SemaphoreType.DMA((1,))],
+        limit=STENCIL_LIMIT,
     )(flip, tangent, velocity, depth, solved)
 
     following, previous = call(

time: 43.2 us -> 43 us (level)
  starting transfers between devices: 23.2 us -> 24.9 us
  waiting for transfers between devices: 4.94 us -> 3.53 us
  local copies, waits for them, and re-layouts: 1.76 us -> 0.71 us
  Pallas kernels: 12.2 us -> 12.8 us
    ppermute x3, starting transfers between devices: 5.85 us -> 7.61 us  [shards(): lax.ppermute(value, both, [(target, source) for source, target in way])]
    ppermute x3, waiting for transfers between devices: 1.42 us -> 0.01 us  [shards(): lax.ppermute(value, both, [(target, source) for source, target in way])]
    unnamed x18 -> x16, local copies, waits for them, and re-layouts: 1.76 us -> 0.71 us
    pallas_call x1, Pallas kernels: 3.3 us -> 3.86 us  [shards(): call(stencil_kernel, 'stencil', 3.0, 'SVVVH', [('V', blocked), ('V', natu...]
  transfers between devices with their start and end apart: 11 -> 11, of which waited for: 4 -> 3; matrix products, arithmetic and copies ran while one was open for 0% -> 0% of each run, Pallas kernels for 22% -> 24%
where the time goes in v4:
time: 43 us; the launch traced here: 42.7 us
  starting transfers between devices  24.9 us (58%)
  Pallas kernels  12.8 us (30%)
  waiting for transfers between devices  3.53 us (8%)
  between operations  0.76 us (2%)
  local copies, waits for them, and re-layouts  0.71 us (2%)
    ppermute x3, starting transfers between devices, shards(): asked = [lax.ppermute(mine, both, way) for way in hops()]  8.31 us
    ppermute x3, starting transfers between devices, shards(): lax.ppermute(value, both, [(target, source) for source, target in way])  7.61 us
    all_to_all x1, starting transfers between devices, shards(): lax.all_to_all(slots, 'tile', 0, 0, axis_index_groups=groups, tiled=True)  4.92 us
    ppermute x4, starting transfers between devices, swap(): return lax.ppermute(value, axis, [(i, i ^ bit) for i in range(size)])  4.1 us
    pallas_call x1, Pallas kernels, shards(): call(stencil_kernel, 'stencil', 3.0, 'SVVVH', [('V', blocked), ('V', natu...  3.86 us
    pallas_call x1, Pallas kernels, shards(): call(solve_kernel, 'solve', 4.0, 'SSHHHHHHH', [('V', (136, 128)), ('V', l...  3.48 us
    pallas_call x1, Pallas kernels, shards(): call(lookup_kernel, 'lookup', 2.7, 'V' * 6, [('V', answer)] * 4, [pltpu.V...  2.73 us
    ppermute x4, waiting for transfers between devices, swap(): return lax.ppermute(value, axis, [(i, i ^ bit) for i in range(size)])  2.7 us
  transfers between devices with their start and end apart: 11, of which 3 were waited for; matrix products, arithmetic and copies ran while one was open for 0% of the time, Pallas kernels for 24%

profile of v4, /device:TPU:6, one launch (start us, length us, event | category | flops | bytes accessed | tf_op | source)
XLA Modules:
  0.0 42.7 jit_solution(3826118952721714827)
XLA Ops:
  0.6 6.8 %collective-permute-start.2 = (s32[1,900]{1,0:T(1,128)}, s32[1,900]{1,0:T(1,128)S(1)}, u32[]{:S(2)}, u32[]{:S(2)}) collective-permute-start(s32[1,900]{1,0:T(1,128)} %bitcast.22), channel_id=1, source_target_pairs={{0,129},{2,131},{4,133},{6,135},{8,137},{10,139},{12,141},{14,143}... | collective-permute-start | bytes 10808 | tf_op jit(solution)/shard_map/ppermute | solution.py:518
  7.5 1.5 %collective-permute-start.1 = (s32[1,900]{1,0:T(1,128)}, s32[1,900]{1,0:T(1,128)S(1)}, u32[]{:S(2)}, u32[]{:S(2)}) collective-permute-start(s32[1,900]{1,0:T(1,128)} %bitcast.23), channel_id=1, source_target_pairs={{0,64},{2,66},{4,68},{6,70},{8,72},{10,74},{12,76},{14,78},{16,80}... | collective-permute-start | bytes 10808 | tf_op jit(solution)/shard_map/ppermute | solution.py:518
  8.9 0.0 collective-permute-start
  9.0 0.7 %copy-done.3 = f32[1,1,2,900]{3,2,1,0:T(2,128)S(1)} copy-done((f32[1,1,2,900]{3,2,1,0:T(2,128)S(1)}, f32[1,1,2,900]{3,2,1,0:T(2,128)}, u32[]{:S(2)}) %copy-start.3) | copy-done | bytes 7224
  9.6 0.0 copy-done.4
  9.7 3.5 %solve.1 = (f32[136,128]{1,0:T(8,128)S(1)}, s32[1,900]{1,0:T(1,128)S(1)}, f32[384,128]{1,0:T(8,128)S(1)}, f32[2,512,128]{2,1,0:T(8,128)}, f32[56,128]{1,0:T(8,128)S(1)}, /*index=5*/f32[1024,128]{1,0:T(8,128)}) custom-call(s32[1,4]{1,0:T(1,128)S(1)} %bitcast.28, s32[1,4]{1,0:T(1,128)S(1)} %bitcast.26, f32[2,64,900]{2,1,0:T(8,128)} %bitcast.29, ...), custom_call_target="tpu_custom_call" | custom-call | bytes 14760000 | tf_op jit(solution)/shard_map/solve/pallas_call | solution.py:520
  13.1 0.2 collective-permute-done.1.q2
  13.4 0.6 %collective-permute-done.q1 = s32[1,900]{1,0:T(1,128)S(1)} collective-permute-done((s32[1,900]{1,0:T(1,128)}, s32[1,900]{1,0:T(1,128)S(1)}, u32[]{:S(2)}, u32[]{:S(2)}) %collective-permute-start) | collective-permute-done | bytes 3632 | tf_op jit(solution)/shard_map/ppermute | solution.py:518
  14.0 3.0 %collective-permute-start.6 = (f32[136,128]{1,0:T(8,128)S(1)}, f32[136,128]{1,0:T(8,128)S(1)}, u32[]{:S(2)}, u32[]{:S(2)}) collective-permute-start(f32[136,128]{1,0:T(8,128)S(1)} %get-tuple-element.33.e0), channel_id=1, source_target_pairs={{0,24},{1,25},{2,26},{3,27},{4,28},{5,29},{6,30},{7,31},{8,16},{9,... | collective-permute-start | bytes 208904 | tf_op jit(solution)/shard_map/ppermute | solution.py:486
  17.0 0.6 %collective-permute-start.5 = (f32[136,128]{1,0:T(8,128)S(1)}, f32[136,128]{1,0:T(8,128)S(1)}, u32[]{:S(2)}, u32[]{:S(2)}) collective-permute-start(f32[136,128]{1,0:T(8,128)S(1)} %get-tuple-element.33.e0), channel_id=1, source_target_pairs={{0,16},{1,17},{2,18},{3,19},{4,20},{5,21},{6,22},{7,23},{8,24},{9,... | collective-permute-start | bytes 208904 | tf_op jit(solution)/shard_map/ppermute | solution.py:486
  17.6 0.5 %collective-permute-start.4 = (f32[136,128]{1,0:T(8,128)S(1)}, f32[136,128]{1,0:T(8,128)S(1)}, u32[]{:S(2)}, u32[]{:S(2)}) collective-permute-start(f32[136,128]{1,0:T(8,128)S(1)} %get-tuple-element.33.e0), channel_id=1, source_target_pairs={{0,8},{1,9},{2,10},{3,11},{4,12},{5,13},{6,14},{7,15},{8,0},{9,1},... | collective-permute-start | bytes 208904 | tf_op jit(solution)/shard_map/ppermute | solution.py:486
  18.1 0.0 collective-permute-done.3.mate_ref
  18.1 2.7 %lookup.1 = (f32[24,128]{1,0:T(8,128)S(1)}, f32[24,128]{1,0:T(8,128)S(1)}, f32[24,128]{1,0:T(8,128)S(1)}, f32[24,128]{1,0:T(8,128)S(1)}) custom-call(f32[384,128]{1,0:T(8,128)S(1)} %get-tuple-element.28.own_ref, f32[384,128]{1,0:T(8,128)S(1)} %collective-permute-done.3.mate_ref, s32[1,900]{1,0:T(1,128)S(1)} %bitcast.25, ...), custom_call_target="tpu_custom_call" | custom-call | bytes 9963000 | tf_op jit(solution)/shard_map/lookup/pallas_call | solution.py:548
  20.8 0.0 collective-permute-done.6.e3
  20.8 2.7 %collective-permute-done.5.e2 = f32[136,128]{1,0:T(8,128)S(1)} collective-permute-done((f32[136,128]{1,0:T(8,128)S(1)}, f32[136,128]{1,0:T(8,128)S(1)}, u32[]{:S(2)}, u32[]{:S(2)}) %collective-permute-start.5) | collective-permute-done | bytes 69664 | tf_op jit(solution)/shard_map/ppermute | solution.py:486
  23.5 0.9 %route.1 = f32[8,128,128]{2,1,0:T(8,128)} custom-call(f32[136,128]{1,0:T(8,128)S(1)} %get-tuple-element.33.e0, f32[136,128]{1,0:T(8,128)S(1)} %collective-permute-done.4.e1, f32[136,128]{1,0:T(8,128)S(1)} %collective-permute-done.5.e2, f32[136,128]{1,0:T(8,128)S(1)} %collective-permute-done.6.e3), custom_call_target="tpu_custom_call" | custom-call | bytes 3321000 | tf_op jit(solution)/shard_map/route/pallas_call | solution.py:562
  24.4 0.0 copy-start
  24.4 0.0 copy-start.1
  24.4 4.9 %all-to-all-start = ((f32[8,128,128]{2,1,0:T(8,128)}), f32[8,128,128]{2,1,0:T(8,128)S(1)}, u32[]{:S(2)}, u32[]{:S(2)}) async-start(f32[8,128,128]{2,1,0:T(8,128)} %route.1), calls=%async_computation | async-start | bytes 1048576 | tf_op jit(solution)/shard_map/all_to_all | solution.py:571
  29.4 4.4 %collective-permute-start.7 = (f32[24,128]{1,0:T(8,128)S(1)}, f32[24,128]{1,0:T(8,128)S(1)}, u32[]{:S(2)}, u32[]{:S(2)}) collective-permute-start(f32[24,128]{1,0:T(8,128)S(1)} %get-tuple-element.41), channel_id=1, source_target_pairs={{129,0},{131,2},{133,4},{135,6},{137,8},{139,10},{141,12},{143,14}... | collective-permute-start | bytes 36872 | tf_op jit(solution)/shard_map/ppermute | solution.py:557
  33.7 1.1 %collective-permute-start.8 = (f32[24,128]{1,0:T(8,128)S(1)}, f32[24,128]{1,0:T(8,128)S(1)}, u32[]{:S(2)}, u32[]{:S(2)}) collective-permute-start(f32[24,128]{1,0:T(8,128)S(1)} %get-tuple-element.42), channel_id=1, source_target_pairs={{64,0},{66,2},{68,4},{70,6},{72,8},{74,10},{76,12},{78,14},{80,16}... | collective-permute-start | bytes 36872 | tf_op jit(solution)/shard_map/ppermute | solution.py:557
  34.8 2.1 %collective-permute-start.9 = (f32[24,128]{1,0:T(8,128)S(1)}, f32[24,128]{1,0:T(8,128)S(1)}, u32[]{:S(2)}, u32[]{:S(2)}) collective-permute-start(f32[24,128]{1,0:T(8,128)S(1)} %get-tuple-element.43), channel_id=1, source_target_pairs={{193,0},{195,2},{197,4},{199,6},{201,8},{203,10},{205,12},{207,14}... | collective-permute-start | bytes 36872 | tf_op jit(solution)/shard_map/ppermute | solution.py:557
  37.0 3.9 %stencil.1 = (f32[2,512,128]{2,1,0:T(8,128)S(1)}, f32[2,64,900]{2,1,0:T(8,128)S(1)}, f32[192,128]{1,0:T(8,128)S(1)}) custom-call(s32[1,4]{1,0:T(1,128)S(1)} %bitcast.27, f32[2,64,900]{2,1,0:T(8,128)S(1)} %bitcast.19, f32[2,64,900]{2,1,0:T(8,128)S(1)} %bitcast.17, s32[1,900]{1,0:T(1,128)S(1)} %get-tuple-element.34.depth_ref, ...), custom_call_target="tpu_custom_call" | custom-call | bytes 11070000 | tf_op jit(solution)/shard_map/stencil/pallas_call | solution.py:573
  40.9 1.8 %finish.1 = (f32[2,64,900]{2,1,0:T(8,128)}, f32[2,64,900]{2,1,0:T(8,128)}) custom-call(f32[8,128,128]{2,1,0:T(8,128)S(1)} %all-to-all-done.edge_ref, f32[2,512,128]{2,1,0:T(8,128)S(1)} %get-tuple-element.36.rhs_ref, f32[2,64,900]{2,1,0:T(8,128)S(1)} %get-tuple-element.37.back_hbm, f32[192,128]{1,0:T(8,128)S(1)} %get-tuple-element.38.rim_ref, ...), custom_call_target="tpu_custom_call" | custom-call | bytes 7749000 | tf_op jit(solution)/shard_map/finish/pallas_call | solution.py:583
  (19 shorter events, 0.0 us)
Async XLA Ops:
  0.6 12.5 %collective-permute-start.2 = (s32[1,900]{1,0:T(1,128)}, s32[1,900]{1,0:T(1,128)S(1)}, u32[]{:S(2)}, u32[]{:S(2)}) collective-permute-start(s32[1,900]{1,0:T(1,128)} %bitcast.22), channel_id=1, source_target_pairs={{0,129},{2,131},{4,133},{6,135},{8,137},{10,139},{12,141},{14,143}... | collective-permute-start | bytes 10808 | tf_op jit(solution)/shard_map/ppermute | solution.py:518
  7.5 5.9 %collective-permute-start.1 = (s32[1,900]{1,0:T(1,128)}, s32[1,900]{1,0:T(1,128)S(1)}, u32[]{:S(2)}, u32[]{:S(2)}) collective-permute-start(s32[1,900]{1,0:T(1,128)} %bitcast.23), channel_id=1, source_target_pairs={{0,64},{2,66},{4,68},{6,70},{8,72},{10,74},{12,76},{14,78},{16,80}... | collective-permute-start | bytes 10808 | tf_op jit(solution)/shard_map/ppermute | solution.py:518
  8.9 5.0 %collective-permute-start = (s32[1,900]{1,0:T(1,128)}, s32[1,900]{1,0:T(1,128)S(1)}, u32[]{:S(2)}, u32[]{:S(2)}) collective-permute-start(s32[1,900]{1,0:T(1,128)} %bitcast.24), channel_id=1, source_target_pairs={{0,193},{2,195},{4,197},{6,199},{8,201},{10,203},{12,205},{14,207}... | collective-permute-start | bytes 10808 | tf_op jit(solution)/shard_map/ppermute | solution.py:518
  8.9 0.7 %copy-start.3 = (f32[1,1,2,900]{3,2,1,0:T(2,128)S(1)}, f32[1,1,2,900]{3,2,1,0:T(2,128)}, u32[]{:S(2)}) copy-start(f32[1,1,2,900]{3,2,1,0:T(2,128)} %param.12) | copy-start | bytes 21604
  8.9 0.7 %copy-start.4 = (s32[1,1,900]{2,1,0:T(1,128)S(1)}, s32[1,1,900]{2,1,0:T(1,128)}, u32[]{:S(2)}) copy-start(s32[1,1,900]{2,1,0:T(1,128)} %param.15) | copy-start | bytes 10804
  8.9 0.7 %copy-start.6 = (s32[1,1,4]{2,1,0:T(1,128)S(1)}, s32[1,1,4]{2,1,0:T(1,128)}, u32[]{:S(2)}) copy-start(s32[1,1,4]{2,1,0:T(1,128)} %param.19) | copy-start | bytes 52
  9.0 0.7 %copy-start.7 = (s32[1,1,4]{2,1,0:T(1,128)S(1)}, s32[1,1,4]{2,1,0:T(1,128)}, u32[]{:S(2)}) copy-start(s32[1,1,4]{2,1,0:T(1,128)} %param.18) | copy-start | bytes 52
  9.7 8.4 %copy-start.5 = (s32[1,1,900]{2,1,0:T(1,128)S(1)}, s32[1,1,900]{2,1,0:T(1,128)}, u32[]{:S(2)}) copy-start(s32[1,1,900]{2,1,0:T(1,128)} %param.17) | copy-start | bytes 10804
  14.0 4.1 %collective-permute-start.3 = (f32[384,128]{1,0:T(8,128)S(1)}, f32[384,128]{1,0:T(8,128)S(1)}, u32[]{:S(2)}, u32[]{:S(2)}) collective-permute-start(f32[384,128]{1,0:T(8,128)S(1)} %get-tuple-element.28.own_ref), channel_id=1, source_target_pairs={{0,32},{32,0},{64,96},{96,64},{128,160},{160,128},{192,224},{224,1... | collective-permute-start | bytes 589832 | tf_op jit(solution)/shard_map/ppermute | solution.py:486
  14.0 6.8 %collective-permute-start.6 = (f32[136,128]{1,0:T(8,128)S(1)}, f32[136,128]{1,0:T(8,128)S(1)}, u32[]{:S(2)}, u32[]{:S(2)}) collective-permute-start(f32[136,128]{1,0:T(8,128)S(1)} %get-tuple-element.33.e0), channel_id=1, source_target_pairs={{0,24},{1,25},{2,26},{3,27},{4,28},{5,29},{6,30},{7,31},{8,16},{9,... | collective-permute-start | bytes 208904 | tf_op jit(solution)/shard_map/ppermute | solution.py:486
  17.0 6.5 %collective-permute-start.5 = (f32[136,128]{1,0:T(8,128)S(1)}, f32[136,128]{1,0:T(8,128)S(1)}, u32[]{:S(2)}, u32[]{:S(2)}) collective-permute-start(f32[136,128]{1,0:T(8,128)S(1)} %get-tuple-element.33.e0), channel_id=1, source_target_pairs={{0,16},{1,17},{2,18},{3,19},{4,20},{5,21},{6,22},{7,23},{8,24},{9,... | collective-permute-start | bytes 208904 | tf_op jit(solution)/shard_map/ppermute | solution.py:486
  17.6 5.9 %collective-permute-start.4 = (f32[136,128]{1,0:T(8,128)S(1)}, f32[136,128]{1,0:T(8,128)S(1)}, u32[]{:S(2)}, u32[]{:S(2)}) collective-permute-start(f32[136,128]{1,0:T(8,128)S(1)} %get-tuple-element.33.e0), channel_id=1, source_target_pairs={{0,8},{1,9},{2,10},{3,11},{4,12},{5,13},{6,14},{7,15},{8,0},{9,1},... | collective-permute-start | bytes 208904 | tf_op jit(solution)/shard_map/ppermute | solution.py:486
  24.4 12.6 %copy-start = (f32[1,1,2,64,900]{4,3,2,1,0:T(8,128)S(1)}, f32[1,1,2,64,900]{4,3,2,1,0:T(8,128)}, u32[]{:S(2)}) copy-start(f32[1,1,2,64,900]{4,3,2,1,0:T(8,128)} %param.13) | copy-start | bytes 1382404
  24.4 12.5 %copy-start.1 = (f32[1,1,2,64,900]{4,3,2,1,0:T(8,128)S(1)}, f32[1,1,2,64,900]{4,3,2,1,0:T(8,128)}, u32[]{:S(2)}) copy-start(f32[1,1,2,64,900]{4,3,2,1,0:T(8,128)} %param.10) | copy-start | bytes 1382404
  24.4 16.4 %all-to-all-start = ((f32[8,128,128]{2,1,0:T(8,128)}), f32[8,128,128]{2,1,0:T(8,128)S(1)}, u32[]{:S(2)}, u32[]{:S(2)}) async-start(f32[8,128,128]{2,1,0:T(8,128)} %route.1), calls=%async_computation | async-start | bytes 1048576 | tf_op jit(solution)/shard_map/all_to_all | solution.py:571
  29.4 11.5 %collective-permute-start.7 = (f32[24,128]{1,0:T(8,128)S(1)}, f32[24,128]{1,0:T(8,128)S(1)}, u32[]{:S(2)}, u32[]{:S(2)}) collective-permute-start(f32[24,128]{1,0:T(8,128)S(1)} %get-tuple-element.41), channel_id=1, source_target_pairs={{129,0},{131,2},{133,4},{135,6},{137,8},{139,10},{141,12},{143,14}... | collective-permute-start | bytes 36872 | tf_op jit(solution)/shard_map/ppermute | solution.py:557
  33.7 7.1 %collective-permute-start.8 = (f32[24,128]{1,0:T(8,128)S(1)}, f32[24,128]{1,0:T(8,128)S(1)}, u32[]{:S(2)}, u32[]{:S(2)}) collective-permute-start(f32[24,128]{1,0:T(8,128)S(1)} %get-tuple-element.42), channel_id=1, source_target_pairs={{64,0},{66,2},{68,4},{70,6},{72,8},{74,10},{76,12},{78,14},{80,16}... | collective-permute-start | bytes 36872 | tf_op jit(solution)/shard_map/ppermute | solution.py:557
  34.8 6.0 %collective-permute-start.9 = (f32[24,128]{1,0:T(8,128)S(1)}, f32[24,128]{1,0:T(8,128)S(1)}, u32[]{:S(2)}, u32[]{:S(2)}) collective-permute-start(f32[24,128]{1,0:T(8,128)S(1)} %get-tuple-element.43), channel_id=1, source_target_pairs={{193,0},{195,2},{197,4},{199,6},{201,8},{203,10},{205,12},{207,14}... | collective-permute-start | bytes 36872 | tf_op jit(solution)/shard_map/ppermute | solution.py:557
  37.0 3.9 %copy-start.2 = (f32[1024,128]{1,0:T(8,128)S(1)}, f32[1024,128]{1,0:T(8,128)}, u32[]{:S(2)}) copy-start(f32[1024,128]{1,0:T(8,128)} %get-tuple-element.40.link_ref) | copy-start | bytes 1572868

commit v5 on v4

--- a/solution.py
+++ b/solution.py
@@ -249,7 +249,7 @@
             edge_ref[pl.ds(pl.multiple_of(64 * t + 8 * i, 8), 8), :] = edges
         return carry
 
-    lax.fori_loop(0, GROUPS, pack, 0, unroll=4)
+    lax.fori_loop(0, GROUPS, pack, 0, unroll=True)
     second = jnp.logical_or(small < 30, jnp.logical_and(small >= 60, small < 90))
     target = jnp.where(
         second,
@@ -515,7 +515,7 @@
     line = jax.ShapeDtypeStruct((1, CELLS), jnp.int32)
     both = ("region", "tile")
 
-    asked = [lax.ppermute(mine, both, way) for way in hops()]
+    asked = [lax.ppermute(mine, both, way) for way in reversed(hops())][::-1]
     banded = forcing.reshape(8, 128, 128).transpose(1, 0, 2).reshape(1024, 128)
     edges, depth, table, solved, peak, link = call(
         solve_kernel,

time: 43 us -> 43 us (level)
  no operation moved by 1% of the time
where the time goes in v5:
time: 43 us; the launch traced here: 42.7 us
  starting transfers between devices  24.9 us (58%)
  Pallas kernels  12.8 us (30%)
  waiting for transfers between devices  3.53 us (8%)
  between operations  0.76 us (2%)
  local copies, waits for them, and re-layouts  0.71 us (2%)
    ppermute x3, starting transfers between devices, shards(): asked = [lax.ppermute(mine, both, way) for way in reversed(hops())][::-1]  8.31 us
    ppermute x3, starting transfers between devices, shards(): lax.ppermute(value, both, [(target, source) for source, target in way])  7.61 us
    all_to_all x1, starting transfers between devices, shards(): lax.all_to_all(slots, 'tile', 0, 0, axis_index_groups=groups, tiled=True)  4.92 us
    ppermute x4, starting transfers between devices, swap(): return lax.ppermute(value, axis, [(i, i ^ bit) for i in range(size)])  4.1 us
    pallas_call x1, Pallas kernels, shards(): call(stencil_kernel, 'stencil', 3.0, 'SVVVH', [('V', blocked), ('V', natu...  3.86 us
    pallas_call x1, Pallas kernels, shards(): call(solve_kernel, 'solve', 4.0, 'SSHHHHHHH', [('V', (136, 128)), ('V', l...  3.48 us
    pallas_call x1, Pallas kernels, shards(): call(lookup_kernel, 'lookup', 2.7, 'V' * 6, [('V', answer)] * 4, [pltpu.V...  2.73 us
    ppermute x4, waiting for transfers between devices, swap(): return lax.ppermute(value, axis, [(i, i ^ bit) for i in range(size)])  2.7 us
  transfers between devices with their start and end apart: 11, of which 3 were waited for; matrix products, arithmetic and copies ran while one was open for 0% of the time, Pallas kernels for 24%

profile of v5, /device:TPU:6, one launch (start us, length us, event | category | flops | bytes accessed | tf_op | source)
XLA Modules:
  0.0 42.7 jit_solution(15421442013052501473)
XLA Ops:
  0.6 6.8 %collective-permute-start.2 = (s32[1,900]{1,0:T(1,128)}, s32[1,900]{1,0:T(1,128)S(1)}, u32[]{:S(2)}, u32[]{:S(2)}) collective-permute-start(s32[1,900]{1,0:T(1,128)} %bitcast.22), channel_id=1, source_target_pairs={{0,129},{2,131},{4,133},{6,135},{8,137},{10,139},{12,141},{14,143}... | collective-permute-start | bytes 10808 | tf_op jit(solution)/shard_map/ppermute | solution.py:518
  7.5 1.5 %collective-permute-start.1 = (s32[1,900]{1,0:T(1,128)}, s32[1,900]{1,0:T(1,128)S(1)}, u32[]{:S(2)}, u32[]{:S(2)}) collective-permute-start(s32[1,900]{1,0:T(1,128)} %bitcast.23), channel_id=1, source_target_pairs={{0,64},{2,66},{4,68},{6,70},{8,72},{10,74},{12,76},{14,78},{16,80}... | collective-permute-start | bytes 10808 | tf_op jit(solution)/shard_map/ppermute | solution.py:518
  8.9 0.0 collective-permute-start
  9.0 0.7 %copy-done.3 = f32[1,1,2,900]{3,2,1,0:T(2,128)S(1)} copy-done((f32[1,1,2,900]{3,2,1,0:T(2,128)S(1)}, f32[1,1,2,900]{3,2,1,0:T(2,128)}, u32[]{:S(2)}) %copy-start.3) | copy-done | bytes 7224
  9.6 0.0 copy-done.4
  9.7 3.5 %solve.1 = (f32[136,128]{1,0:T(8,128)S(1)}, s32[1,900]{1,0:T(1,128)S(1)}, f32[384,128]{1,0:T(8,128)S(1)}, f32[2,512,128]{2,1,0:T(8,128)}, f32[56,128]{1,0:T(8,128)S(1)}, /*index=5*/f32[1024,128]{1,0:T(8,128)}) custom-call(s32[1,4]{1,0:T(1,128)S(1)} %bitcast.28, s32[1,4]{1,0:T(1,128)S(1)} %bitcast.26, f32[2,64,900]{2,1,0:T(8,128)} %bitcast.29, ...), custom_call_target="tpu_custom_call" | custom-call | bytes 14760000 | tf_op jit(solution)/shard_map/solve/pallas_call | solution.py:520
  13.1 0.2 collective-permute-done.1.q2
  13.4 0.6 %collective-permute-done.q1 = s32[1,900]{1,0:T(1,128)S(1)} collective-permute-done((s32[1,900]{1,0:T(1,128)}, s32[1,900]{1,0:T(1,128)S(1)}, u32[]{:S(2)}, u32[]{:S(2)}) %collective-permute-start) | collective-permute-done | bytes 3632 | tf_op jit(solution)/shard_map/ppermute | solution.py:518
  14.0 3.0 %collective-permute-start.6 = (f32[136,128]{1,0:T(8,128)S(1)}, f32[136,128]{1,0:T(8,128)S(1)}, u32[]{:S(2)}, u32[]{:S(2)}) collective-permute-start(f32[136,128]{1,0:T(8,128)S(1)} %get-tuple-element.33.e0), channel_id=1, source_target_pairs={{0,24},{1,25},{2,26},{3,27},{4,28},{5,29},{6,30},{7,31},{8,16},{9,... | collective-permute-start | bytes 208904 | tf_op jit(solution)/shard_map/ppermute | solution.py:486
  17.0 0.6 %collective-permute-start.5 = (f32[136,128]{1,0:T(8,128)S(1)}, f32[136,128]{1,0:T(8,128)S(1)}, u32[]{:S(2)}, u32[]{:S(2)}) collective-permute-start(f32[136,128]{1,0:T(8,128)S(1)} %get-tuple-element.33.e0), channel_id=1, source_target_pairs={{0,16},{1,17},{2,18},{3,19},{4,20},{5,21},{6,22},{7,23},{8,24},{9,... | collective-permute-start | bytes 208904 | tf_op jit(solution)/shard_map/ppermute | solution.py:486
  17.6 0.5 %collective-permute-start.4 = (f32[136,128]{1,0:T(8,128)S(1)}, f32[136,128]{1,0:T(8,128)S(1)}, u32[]{:S(2)}, u32[]{:S(2)}) collective-permute-start(f32[136,128]{1,0:T(8,128)S(1)} %get-tuple-element.33.e0), channel_id=1, source_target_pairs={{0,8},{1,9},{2,10},{3,11},{4,12},{5,13},{6,14},{7,15},{8,0},{9,1},... | collective-permute-start | bytes 208904 | tf_op jit(solution)/shard_map/ppermute | solution.py:486
  18.1 0.0 collective-permute-done.3.mate_ref
  18.1 2.7 %lookup.1 = (f32[24,128]{1,0:T(8,128)S(1)}, f32[24,128]{1,0:T(8,128)S(1)}, f32[24,128]{1,0:T(8,128)S(1)}, f32[24,128]{1,0:T(8,128)S(1)}) custom-call(f32[384,128]{1,0:T(8,128)S(1)} %get-tuple-element.28.own_ref, f32[384,128]{1,0:T(8,128)S(1)} %collective-permute-done.3.mate_ref, s32[1,900]{1,0:T(1,128)S(1)} %bitcast.25, ...), custom_call_target="tpu_custom_call" | custom-call | bytes 9963000 | tf_op jit(solution)/shard_map/lookup/pallas_call | solution.py:548
  20.8 0.0 collective-permute-done.6.e3
  20.8 2.7 %collective-permute-done.5.e2 = f32[136,128]{1,0:T(8,128)S(1)} collective-permute-done((f32[136,128]{1,0:T(8,128)S(1)}, f32[136,128]{1,0:T(8,128)S(1)}, u32[]{:S(2)}, u32[]{:S(2)}) %collective-permute-start.5) | collective-permute-done | bytes 69664 | tf_op jit(solution)/shard_map/ppermute | solution.py:486
  23.5 0.9 %route.1 = f32[8,128,128]{2,1,0:T(8,128)} custom-call(f32[136,128]{1,0:T(8,128)S(1)} %get-tuple-element.33.e0, f32[136,128]{1,0:T(8,128)S(1)} %collective-permute-done.4.e1, f32[136,128]{1,0:T(8,128)S(1)} %collective-permute-done.5.e2, f32[136,128]{1,0:T(8,128)S(1)} %collective-permute-done.6.e3), custom_call_target="tpu_custom_call" | custom-call | bytes 3321000 | tf_op jit(solution)/shard_map/route/pallas_call | solution.py:562
  24.4 0.0 copy-start
  24.4 0.0 copy-start.1
  24.4 4.9 %all-to-all-start = ((f32[8,128,128]{2,1,0:T(8,128)}), f32[8,128,128]{2,1,0:T(8,128)S(1)}, u32[]{:S(2)}, u32[]{:S(2)}) async-start(f32[8,128,128]{2,1,0:T(8,128)} %route.1), calls=%async_computation | async-start | bytes 1048576 | tf_op jit(solution)/shard_map/all_to_all | solution.py:571
  29.4 4.4 %collective-permute-start.7 = (f32[24,128]{1,0:T(8,128)S(1)}, f32[24,128]{1,0:T(8,128)S(1)}, u32[]{:S(2)}, u32[]{:S(2)}) collective-permute-start(f32[24,128]{1,0:T(8,128)S(1)} %get-tuple-element.41), channel_id=1, source_target_pairs={{129,0},{131,2},{133,4},{135,6},{137,8},{139,10},{141,12},{143,14}... | collective-permute-start | bytes 36872 | tf_op jit(solution)/shard_map/ppermute | solution.py:557
  33.7 1.1 %collective-permute-start.8 = (f32[24,128]{1,0:T(8,128)S(1)}, f32[24,128]{1,0:T(8,128)S(1)}, u32[]{:S(2)}, u32[]{:S(2)}) collective-permute-start(f32[24,128]{1,0:T(8,128)S(1)} %get-tuple-element.42), channel_id=1, source_target_pairs={{64,0},{66,2},{68,4},{70,6},{72,8},{74,10},{76,12},{78,14},{80,16}... | collective-permute-start | bytes 36872 | tf_op jit(solution)/shard_map/ppermute | solution.py:557
  34.8 2.1 %collective-permute-start.9 = (f32[24,128]{1,0:T(8,128)S(1)}, f32[24,128]{1,0:T(8,128)S(1)}, u32[]{:S(2)}, u32[]{:S(2)}) collective-permute-start(f32[24,128]{1,0:T(8,128)S(1)} %get-tuple-element.43), channel_id=1, source_target_pairs={{193,0},{195,2},{197,4},{199,6},{201,8},{203,10},{205,12},{207,14}... | collective-permute-start | bytes 36872 | tf_op jit(solution)/shard_map/ppermute | solution.py:557
  37.0 3.9 %stencil.1 = (f32[2,512,128]{2,1,0:T(8,128)S(1)}, f32[2,64,900]{2,1,0:T(8,128)S(1)}, f32[192,128]{1,0:T(8,128)S(1)}) custom-call(s32[1,4]{1,0:T(1,128)S(1)} %bitcast.27, f32[2,64,900]{2,1,0:T(8,128)S(1)} %bitcast.19, f32[2,64,900]{2,1,0:T(8,128)S(1)} %bitcast.17, s32[1,900]{1,0:T(1,128)S(1)} %get-tuple-element.34.depth_ref, ...), custom_call_target="tpu_custom_call" | custom-call | bytes 11070000 | tf_op jit(solution)/shard_map/stencil/pallas_call | solution.py:573
  40.9 1.8 %finish.1 = (f32[2,64,900]{2,1,0:T(8,128)}, f32[2,64,900]{2,1,0:T(8,128)}) custom-call(f32[8,128,128]{2,1,0:T(8,128)S(1)} %all-to-all-done.edge_ref, f32[2,512,128]{2,1,0:T(8,128)S(1)} %get-tuple-element.36.rhs_ref, f32[2,64,900]{2,1,0:T(8,128)S(1)} %get-tuple-element.37.back_hbm, f32[192,128]{1,0:T(8,128)S(1)} %get-tuple-element.38.rim_ref, ...), custom_call_target="tpu_custom_call" | custom-call | bytes 7749000 | tf_op jit(solution)/shard_map/finish/pallas_call | solution.py:583
  (19 shorter events, 0.0 us)
Async XLA Ops:
  0.6 12.5 %collective-permute-start.2 = (s32[1,900]{1,0:T(1,128)}, s32[1,900]{1,0:T(1,128)S(1)}, u32[]{:S(2)}, u32[]{:S(2)}) collective-permute-start(s32[1,900]{1,0:T(1,128)} %bitcast.22), channel_id=1, source_target_pairs={{0,129},{2,131},{4,133},{6,135},{8,137},{10,139},{12,141},{14,143}... | collective-permute-start | bytes 10808 | tf_op jit(solution)/shard_map/ppermute | solution.py:518
  7.5 5.9 %collective-permute-start.1 = (s32[1,900]{1,0:T(1,128)}, s32[1,900]{1,0:T(1,128)S(1)}, u32[]{:S(2)}, u32[]{:S(2)}) collective-permute-start(s32[1,900]{1,0:T(1,128)} %bitcast.23), channel_id=1, source_target_pairs={{0,64},{2,66},{4,68},{6,70},{8,72},{10,74},{12,76},{14,78},{16,80}... | collective-permute-start | bytes 10808 | tf_op jit(solution)/shard_map/ppermute | solution.py:518
  8.9 5.0 %collective-permute-start = (s32[1,900]{1,0:T(1,128)}, s32[1,900]{1,0:T(1,128)S(1)}, u32[]{:S(2)}, u32[]{:S(2)}) collective-permute-start(s32[1,900]{1,0:T(1,128)} %bitcast.24), channel_id=1, source_target_pairs={{0,193},{2,195},{4,197},{6,199},{8,201},{10,203},{12,205},{14,207}... | collective-permute-start | bytes 10808 | tf_op jit(solution)/shard_map/ppermute | solution.py:518
  8.9 0.7 %copy-start.3 = (f32[1,1,2,900]{3,2,1,0:T(2,128)S(1)}, f32[1,1,2,900]{3,2,1,0:T(2,128)}, u32[]{:S(2)}) copy-start(f32[1,1,2,900]{3,2,1,0:T(2,128)} %param.12) | copy-start | bytes 21604
  8.9 0.7 %copy-start.4 = (s32[1,1,900]{2,1,0:T(1,128)S(1)}, s32[1,1,900]{2,1,0:T(1,128)}, u32[]{:S(2)}) copy-start(s32[1,1,900]{2,1,0:T(1,128)} %param.15) | copy-start | bytes 10804
  8.9 0.7 %copy-start.6 = (s32[1,1,4]{2,1,0:T(1,128)S(1)}, s32[1,1,4]{2,1,0:T(1,128)}, u32[]{:S(2)}) copy-start(s32[1,1,4]{2,1,0:T(1,128)} %param.19) | copy-start | bytes 52
  9.0 0.7 %copy-start.7 = (s32[1,1,4]{2,1,0:T(1,128)S(1)}, s32[1,1,4]{2,1,0:T(1,128)}, u32[]{:S(2)}) copy-start(s32[1,1,4]{2,1,0:T(1,128)} %param.18) | copy-start | bytes 52
  9.7 8.4 %copy-start.5 = (s32[1,1,900]{2,1,0:T(1,128)S(1)}, s32[1,1,900]{2,1,0:T(1,128)}, u32[]{:S(2)}) copy-start(s32[1,1,900]{2,1,0:T(1,128)} %param.17) | copy-start | bytes 10804
  14.0 4.1 %collective-permute-start.3 = (f32[384,128]{1,0:T(8,128)S(1)}, f32[384,128]{1,0:T(8,128)S(1)}, u32[]{:S(2)}, u32[]{:S(2)}) collective-permute-start(f32[384,128]{1,0:T(8,128)S(1)} %get-tuple-element.28.own_ref), channel_id=1, source_target_pairs={{0,32},{32,0},{64,96},{96,64},{128,160},{160,128},{192,224},{224,1... | collective-permute-start | bytes 589832 | tf_op jit(solution)/shard_map/ppermute | solution.py:486
  14.0 6.8 %collective-permute-start.6 = (f32[136,128]{1,0:T(8,128)S(1)}, f32[136,128]{1,0:T(8,128)S(1)}, u32[]{:S(2)}, u32[]{:S(2)}) collective-permute-start(f32[136,128]{1,0:T(8,128)S(1)} %get-tuple-element.33.e0), channel_id=1, source_target_pairs={{0,24},{1,25},{2,26},{3,27},{4,28},{5,29},{6,30},{7,31},{8,16},{9,... | collective-permute-start | bytes 208904 | tf_op jit(solution)/shard_map/ppermute | solution.py:486
  17.0 6.5 %collective-permute-start.5 = (f32[136,128]{1,0:T(8,128)S(1)}, f32[136,128]{1,0:T(8,128)S(1)}, u32[]{:S(2)}, u32[]{:S(2)}) collective-permute-start(f32[136,128]{1,0:T(8,128)S(1)} %get-tuple-element.33.e0), channel_id=1, source_target_pairs={{0,16},{1,17},{2,18},{3,19},{4,20},{5,21},{6,22},{7,23},{8,24},{9,... | collective-permute-start | bytes 208904 | tf_op jit(solution)/shard_map/ppermute | solution.py:486
  17.6 5.9 %collective-permute-start.4 = (f32[136,128]{1,0:T(8,128)S(1)}, f32[136,128]{1,0:T(8,128)S(1)}, u32[]{:S(2)}, u32[]{:S(2)}) collective-permute-start(f32[136,128]{1,0:T(8,128)S(1)} %get-tuple-element.33.e0), channel_id=1, source_target_pairs={{0,8},{1,9},{2,10},{3,11},{4,12},{5,13},{6,14},{7,15},{8,0},{9,1},... | collective-permute-start | bytes 208904 | tf_op jit(solution)/shard_map/ppermute | solution.py:486
  24.4 12.6 %copy-start = (f32[1,1,2,64,900]{4,3,2,1,0:T(8,128)S(1)}, f32[1,1,2,64,900]{4,3,2,1,0:T(8,128)}, u32[]{:S(2)}) copy-start(f32[1,1,2,64,900]{4,3,2,1,0:T(8,128)} %param.13) | copy-start | bytes 1382404
  24.4 12.5 %copy-start.1 = (f32[1,1,2,64,900]{4,3,2,1,0:T(8,128)S(1)}, f32[1,1,2,64,900]{4,3,2,1,0:T(8,128)}, u32[]{:S(2)}) copy-start(f32[1,1,2,64,900]{4,3,2,1,0:T(8,128)} %param.10) | copy-start | bytes 1382404
  24.4 16.4 %all-to-all-start = ((f32[8,128,128]{2,1,0:T(8,128)}), f32[8,128,128]{2,1,0:T(8,128)S(1)}, u32[]{:S(2)}, u32[]{:S(2)}) async-start(f32[8,128,128]{2,1,0:T(8,128)} %route.1), calls=%async_computation | async-start | bytes 1048576 | tf_op jit(solution)/shard_map/all_to_all | solution.py:571
  29.4 11.5 %collective-permute-start.7 = (f32[24,128]{1,0:T(8,128)S(1)}, f32[24,128]{1,0:T(8,128)S(1)}, u32[]{:S(2)}, u32[]{:S(2)}) collective-permute-start(f32[24,128]{1,0:T(8,128)S(1)} %get-tuple-element.41), channel_id=1, source_target_pairs={{129,0},{131,2},{133,4},{135,6},{137,8},{139,10},{141,12},{143,14}... | collective-permute-start | bytes 36872 | tf_op jit(solution)/shard_map/ppermute | solution.py:557
  33.7 7.1 %collective-permute-start.8 = (f32[24,128]{1,0:T(8,128)S(1)}, f32[24,128]{1,0:T(8,128)S(1)}, u32[]{:S(2)}, u32[]{:S(2)}) collective-permute-start(f32[24,128]{1,0:T(8,128)S(1)} %get-tuple-element.42), channel_id=1, source_target_pairs={{64,0},{66,2},{68,4},{70,6},{72,8},{74,10},{76,12},{78,14},{80,16}... | collective-permute-start | bytes 36872 | tf_op jit(solution)/shard_map/ppermute | solution.py:557
  34.8 6.0 %collective-permute-start.9 = (f32[24,128]{1,0:T(8,128)S(1)}, f32[24,128]{1,0:T(8,128)S(1)}, u32[]{:S(2)}, u32[]{:S(2)}) collective-permute-start(f32[24,128]{1,0:T(8,128)S(1)} %get-tuple-element.43), channel_id=1, source_target_pairs={{193,0},{195,2},{197,4},{199,6},{201,8},{203,10},{205,12},{207,14}... | collective-permute-start | bytes 36872 | tf_op jit(solution)/shard_map/ppermute | solution.py:557
  37.0 3.9 %copy-start.2 = (f32[1024,128]{1,0:T(8,128)S(1)}, f32[1024,128]{1,0:T(8,128)}, u32[]{:S(2)}) copy-start(f32[1024,128]{1,0:T(8,128)} %get-tuple-element.40.link_ref) | copy-start | bytes 1572868
